TPU v7x, 128 devices: a whole 4x4x4 slice. The times are simulated.
128 devices in a mesh: dp: 16 (over y, x), samp: 4 (over z_lo, core), col: 2 (over z_hi).
Axes of the slice: x: 4, y: 4, z: 4 (z_hi: 2, z_lo: 2; z = z_hi * 2 + z_lo), core: 2. Of those that a mesh axis runs over, the one named last changes fastest.
Arguments:
- looked_rows: bfloat16 [64, 1920, 128], P(('dp', 'samp'), None, 'col'), may hold values from -6 to 6
- bag_ids: int32 [64, 1920], P(('dp', 'samp')), may hold values from 0 to 959, never falling along the last dimension, each value on 1 to 4 neighbouring positions
- slot_of: int32 [40], replicated, may hold values from 0 to 39, each once
- labels: int32 [1536], P(('dp', 'samp')), may hold values 0 or 1
- out_weight: bfloat16 [3, 128], replicated, may hold values from -0.02734375 to 0.02734375
- filter_first: bfloat16 [128, 1521], replicated, may hold values from -0.15625 to 0.15625
- filter_second: bfloat16 [128, 4992], replicated, may hold values from -0.078125 to 0.078125
- filter_third: bfloat16 [128, 4992], replicated, may hold values from -0.078125 to 0.078125
Outputs:
- row_grads: bfloat16 [64, 1920, 128], P(('dp', 'samp'), None, 'col')
- grad_first: float32 [128, 1521], P('dp')
- grad_second: float32 [128, 4992], P('dp')
- grad_third: float32 [128, 4992], P('dp')
Inputs may be any that keep to these rules, and one draw needn't show every extreme that they name: `bag_ids`: within each owner's row, bag numbers never fall; each of the 960 bags has 1 to 4 entries and some bag exactly 4. `slot_of`: each slot number once.
All inputs are finite; a program needn't handle non-finite values. No bound on the sum of `labels` on one device may be relied on, other than what follows from the above.
Results may differ from a plain program's by a relative error of at most 0.014.
Values may be sent and summed in bfloat16 or wider, within the bound.
A program may use at most 64 MiB of HBM per device.

v0:
```python
import jax
import jax.numpy as jnp
from jax import lax
from jax.sharding import PartitionSpec as P

FIELDS = 39


loss_scale = 16.0
block_rows = 4


def from_everyone(array, axis):
    size = lax.axis_size(axis)
    return lax.all_to_all(
        jnp.broadcast_to(array[None], (size, *array.shape)), axis, 0, 0, tiled=True
    )


def taken_together(array, axis):
    everything = from_everyone(array, axis)
    return jnp.sum(everything, axis=0)


def in_one(arrays, axis):
    ends = [0]
    for a in arrays:
        ends.append(ends[-1] + a.size)
    running = taken_together(jnp.concatenate([a.ravel() for a in arrays]), axis)
    return tuple((running[b:e].reshape(a.shape) for a, b, e in zip(arrays, ends, ends[1:])))


def outer_block(previous, anchor):
    spread_rows = previous.astype(jnp.float32)[:, None, :] * anchor.astype(jnp.float32)[None, :, :]
    return spread_rows.astype(jnp.bfloat16)


def forward_layer(filter_cube, previous, anchor):

    def one_block(operands):
        outer_products = outer_block(operands[0], operands[1])
        projected_maps = jnp.einsum(
            "ocf,cfl->ol", filter_cube, outer_products, preferred_element_type=jnp.float32
        )
        return projected_maps.astype(jnp.bfloat16)

    return lax.map(one_block, (previous, anchor))


def backward_layer(filter_cube, cotangent, previous, anchor):

    def accumulate(running, operands):
        cotangent_part, previous_block, anchor_block = operands
        outer_products = outer_block(previous_block, anchor_block)
        running = running + jnp.einsum(
            "ol,cfl->ocf", cotangent_part, outer_products, preferred_element_type=jnp.float32
        )
        spread_rows = jnp.einsum(
            "ocf,ol->cfl", filter_cube, cotangent_part, preferred_element_type=jnp.float32
        )
        grad_previous = jnp.sum(spread_rows * anchor_block.astype(jnp.float32)[None, :, :], axis=1)
        grad_anchor = jnp.sum(spread_rows * previous_block.astype(jnp.float32)[:, None, :], axis=0)
        return (running, (grad_previous, grad_anchor))

    starting = jnp.zeros(filter_cube.shape, jnp.float32)
    running, (grad_previous, grad_anchor) = lax.scan(
        accumulate, starting, (cotangent, previous, anchor)
    )
    return (
        running.reshape(filter_cube.shape[0], filter_cube.shape[1] * filter_cube.shape[2]),
        grad_previous,
        grad_anchor,
    )


def local(
    looked_rows, bag_ids, slot_of, labels, out_weight, filter_first, filter_second, filter_third
):
    samples = labels.shape[0]
    slots = slot_of.shape[0]
    bag_count = samples * slots
    owners = lax.axis_size("samp")
    group_size = samples * owners
    slot_span = slots // owners
    blocks = samples // block_rows
    entries = bag_ids[0]
    member = (entries[None, :] == jnp.arange(bag_count, dtype=jnp.int32)[:, None]).astype(
        jnp.bfloat16
    )
    pooled = jnp.dot(member, looked_rows[0], preferred_element_type=jnp.float32).astype(
        jnp.bfloat16
    )
    width = pooled.shape[1]
    lanes = block_rows * width
    pooled = pooled.reshape(group_size, slot_span, width)
    arrived = lax.all_to_all(pooled, "samp", split_axis=0, concat_axis=1, tiled=True)
    chooser = (slot_of[:FIELDS][:, None] == jnp.arange(slots, dtype=jnp.int32)[None, :]).astype(
        jnp.bfloat16
    )
    arrived_blocks = arrived.reshape(blocks, block_rows, slots, width)
    anchor = jnp.einsum(
        "fk,nbkd->nfbd", chooser, arrived_blocks, preferred_element_type=jnp.float32
    ).astype(jnp.bfloat16)
    anchor = anchor.reshape(blocks, FIELDS, lanes)
    cube_first = filter_first.reshape(filter_first.shape[0], FIELDS, FIELDS)
    cube_second = filter_second.reshape(
        filter_second.shape[0], filter_second.shape[1] // FIELDS, FIELDS
    )
    cube_third = filter_third.reshape(
        filter_third.shape[0], filter_third.shape[1] // FIELDS, FIELDS
    )
    maps_count = filter_first.shape[0]
    layer_one = forward_layer(cube_first, anchor, anchor)
    layer_two = forward_layer(cube_second, layer_one, anchor)
    layer_three = forward_layer(cube_third, layer_two, anchor)

    def column_sums(layer):
        summed = jnp.sum(
            layer.astype(jnp.float32).reshape(blocks, maps_count, block_rows, width), axis=3
        )
        return summed.transpose(0, 2, 1).reshape(samples, maps_count)

    maps_one, maps_two, maps_three = in_one(
        (column_sums(layer_one), column_sums(layer_two), column_sums(layer_three)), "col"
    )
    weights_out = out_weight.astype(jnp.float32)
    logits = jnp.dot(maps_one, weights_out[0], precision=lax.Precision.HIGHEST)
    logits = logits + jnp.dot(maps_two, weights_out[1], precision=lax.Precision.HIGHEST)
    logits = logits + jnp.dot(maps_three, weights_out[2], precision=lax.Precision.HIGHEST)
    residual_slope = loss_scale * (jax.nn.sigmoid(logits) - labels.astype(jnp.float32))

    def direct_term(weight_row):
        scaled = (residual_slope[:, None] * weight_row[None, :]).reshape(
            blocks, block_rows, maps_count
        )
        scaled = scaled.transpose(0, 2, 1)[:, :, :, None]
        return jnp.broadcast_to(scaled, (blocks, maps_count, block_rows, width)).reshape(
            blocks, maps_count, lanes
        )

    cotan_three = direct_term(weights_out[2]).astype(jnp.bfloat16)
    grad_three, back_two, base_three = backward_layer(cube_third, cotan_three, layer_two, anchor)
    cotan_two = (direct_term(weights_out[1]) + back_two).astype(jnp.bfloat16)
    grad_two, back_one, base_two = backward_layer(cube_second, cotan_two, layer_one, anchor)
    cotan_one = (direct_term(weights_out[0]) + back_one).astype(jnp.bfloat16)
    grad_one, back_zero, base_one = backward_layer(cube_first, cotan_one, anchor, anchor)
    grad_fields = (back_zero + base_one + base_two + base_three).astype(jnp.bfloat16)
    grad_fields = grad_fields.reshape(blocks, FIELDS, block_rows, width)
    slot_grads = jnp.einsum(
        "fk,nfbd->nbkd", chooser, grad_fields, preferred_element_type=jnp.float32
    ).astype(jnp.bfloat16)
    slot_grads = slot_grads.reshape(samples, slots, width)
    returned = lax.all_to_all(slot_grads, "samp", split_axis=1, concat_axis=0, tiled=True)
    bag_grads = returned.reshape(bag_count, width)
    row_grads = jnp.einsum(
        "be,bd->ed", member, bag_grads, preferred_element_type=jnp.float32
    ).astype(jnp.bfloat16)
    summed = lax.psum((grad_one, grad_two, grad_three), ("dp", "samp", "col"))
    share_rows = grad_one.shape[0] // lax.axis_size("dp")
    offset = lax.axis_index("dp") * share_rows
    summed = tuple(
        (lax.dynamic_slice_in_dim(member_sum, offset, share_rows, 0) for member_sum in summed)
    )
    return (row_grads[None], summed[0], summed[1], summed[2])


def solution(mesh):
    in_specs = (
        P(("dp", "samp"), None, "col"),
        P(("dp", "samp"), None),
        P(),
        P(("dp", "samp")),
        P(),
        P(),
        P(),
        P(),
    )
    out_specs = (P(("dp", "samp"), None, "col"), P("dp", None), P("dp", None), P("dp", None))
    return jax.shard_map(local, mesh=mesh, in_specs=in_specs, out_specs=out_specs, check_vma=False)
```

profile of v0, /device:TPU:1, one launch (start us, length us, event | category | flops | bytes accessed | tf_op | source)
XLA Modules:
  0.0 410.3 jit_solution(8385238099146649310)
XLA Ops:
  10.8 4.7 %all-to-all-start = ((bf16[4,2,7680]{2,1,0:T(2,128)(2,1)}), bf16[4,2,7680]{2,1,0:T(2,128)(2,1)S(1)}, u32[]{:S(2)}, u32[]{:S(2)}) async-start(bf16[4,2,7680]{2,1,0:T(2,128)(2,1)} %reshape.239), calls=%async_computation | async-start | bytes 245760 | tf_op jit(solution)/shard_map/all_to_all | solution.py:96
  26.7 3.0 while.75
  29.9 17.4 %while.76 = (s32[]{:T(128)}, bf16[6,128,256]{1,2,0:T(8,128)(2,1)S(1)}, bf16[6,128,256]{1,2,0:T(8,128)(2,1)S(1)}, bf16[6,39,256]{2,1,0:T(8,128)(2,1)S(1)}, bf16[128,128,39]{1,0,2:T(8,128)(2,1)}, /*index=5*/s32[]{:T(128)}) while((s32[]{:T(128)}, bf16[6,128,256]{1,2,0:T(8,128)(2,1)S(1)}, bf16[6,128,256]{1,2,0:T(8,128)(2,1)S(1)}, ...), condition=%wide.region_4.5_spmd, body=%wide.region_3.4_spmd.sunk | while | flops 329787136 | bytes 1772121 | solution.py:47
  29.9 2.8 fusion.111
  32.8 2.8 fusion.111
  35.7 2.8 fusion.111
  38.6 2.8 fusion.111
  41.5 2.8 fusion.111
  44.4 2.8 fusion.111
  47.4 17.4 %while.77 = (s32[]{:T(128)}, bf16[6,128,256]{1,2,0:T(8,128)(2,1)S(1)}, bf16[6,128,256]{1,2,0:T(8,128)(2,1)S(1)}, bf16[6,39,256]{2,1,0:T(8,128)(2,1)S(1)}, bf16[128,128,39]{1,0,2:T(8,128)(2,1)}, /*index=5*/s32[]{:T(128)}) while((s32[]{:T(128)}, bf16[6,128,256]{1,2,0:T(8,128)(2,1)S(1)}, bf16[6,128,256]{1,2,0:T(8,128)(2,1)S(1)}, ...), condition=%wide.region_7.8_spmd, body=%wide.region_6.7_spmd.sunk | while | flops 329787136 | bytes 1772121 | solution.py:47
  47.5 2.8 fusion.113
  50.4 2.8 fusion.113
  53.3 2.8 fusion.113
  56.2 2.8 fusion.113
  61.9 2.8 fusion.113
  65.6 4.9 %all-to-all-start.1 = ((f32[2,1,9216]{2,1,0:T(1,128)}), f32[2,1,9216]{2,1,0:T(1,128)S(1)}, u32[]{:S(2)}, u32[]{:S(2)}) async-start(f32[2,1,9216]{2,1,0:T(1,128)} %broadcast_in_dim.57), calls=%async_computation.1 | async-start | bytes 147456 | tf_op jit(solution)/shard_map/all_to_all | solution.py:15
  78.8 60.0 %while.78 = (s32[]{:T(128)}, f32[128,128,39]{1,0,2:T(8,128)}, f32[6,128,256]{1,2,0:T(8,128)}, f32[6,39,256]{2,1,0:T(8,128)}, bf16[6,128,256]{1,2,0:T(8,128)(2,1)...) while((s32[]{:T(128)}, f32[128,128,39]{1,0,2:T(8,128)}, ...), condition=%wide.region_13.14_spmd.clone, body=%wide.region_10.13_spmd.clone.sunk | while | flops 663257088 | bytes 13269675 | solution.py:66
  79.8 3.4 select_add_fusion.4
  89.1 4.3 %select_add_fusion.4 = f32[128,128,39]{1,0,2:T(8,128)} fusion(f32[128,128,39]{1,0,2:T(8,128)} %get-tuple-element.833, f32[39,256]{1,0:T(8,128)S(1)} %bitcast_convert_fusion.25, f32[128,256]{1,0:T(8,128)S(1)} %bitcast_convert_fusion.26, pred[]{:T(512)S(6)} %compare.9, bf16[6,128,256]{1,2,0:T(8,128)(2,1)} %get-tuple-element.846, s32[]{:T(128)S(6)} %copy.166), kind=kOutput, calls=%fused_computation.34.clone.1 | convolution fusion | flops 330989568 | bytes 5348357 | tf_op jit(solution)/shard_map/while/body/eval_jaxpr/ol,cfl->ocf/dot_general | solution.py:55
  99.2 4.3 %select_add_fusion.4 = f32[128,128,39]{1,0,2:T(8,128)} fusion(f32[128,128,39]{1,0,2:T(8,128)} %get-tuple-element.833, f32[39,256]{1,0:T(8,128)S(1)} %bitcast_convert_fusion.25, f32[128,256]{1,0:T(8,128)S(1)} %bitcast_convert_fusion.26, pred[]{:T(512)S(6)} %compare.9, bf16[6,128,256]{1,2,0:T(8,128)(2,1)} %get-tuple-element.846, s32[]{:T(128)S(6)} %copy.166), kind=kOutput, calls=%fused_computation.34.clone.1 | convolution fusion | flops 330989568 | bytes 5348357 | tf_op jit(solution)/shard_map/while/body/eval_jaxpr/ol,cfl->ocf/dot_general | solution.py:55
  109.4 4.3 %select_add_fusion.4 = f32[128,128,39]{1,0,2:T(8,128)} fusion(f32[128,128,39]{1,0,2:T(8,128)} %get-tuple-element.833, f32[39,256]{1,0:T(8,128)S(1)} %bitcast_convert_fusion.25, f32[128,256]{1,0:T(8,128)S(1)} %bitcast_convert_fusion.26, pred[]{:T(512)S(6)} %compare.9, bf16[6,128,256]{1,2,0:T(8,128)(2,1)} %get-tuple-element.846, s32[]{:T(128)S(6)} %copy.166), kind=kOutput, calls=%fused_computation.34.clone.1 | convolution fusion | flops 330989568 | bytes 5348357 | tf_op jit(solution)/shard_map/while/body/eval_jaxpr/ol,cfl->ocf/dot_general | solution.py:55
  119.5 4.3 %select_add_fusion.4 = f32[128,128,39]{1,0,2:T(8,128)} fusion(f32[128,128,39]{1,0,2:T(8,128)} %get-tuple-element.833, f32[39,256]{1,0:T(8,128)S(1)} %bitcast_convert_fusion.25, f32[128,256]{1,0:T(8,128)S(1)} %bitcast_convert_fusion.26, pred[]{:T(512)S(6)} %compare.9, bf16[6,128,256]{1,2,0:T(8,128)(2,1)} %get-tuple-element.846, s32[]{:T(128)S(6)} %copy.166), kind=kOutput, calls=%fused_computation.34.clone.1 | convolution fusion | flops 330989568 | bytes 5348357 | tf_op jit(solution)/shard_map/while/body/eval_jaxpr/ol,cfl->ocf/dot_general | solution.py:55
  129.7 4.3 %select_add_fusion.4 = f32[128,128,39]{1,0,2:T(8,128)} fusion(f32[128,128,39]{1,0,2:T(8,128)} %get-tuple-element.833, f32[39,256]{1,0:T(8,128)S(1)} %bitcast_convert_fusion.25, f32[128,256]{1,0:T(8,128)S(1)} %bitcast_convert_fusion.26, pred[]{:T(512)S(6)} %compare.9, bf16[6,128,256]{1,2,0:T(8,128)(2,1)} %get-tuple-element.846, s32[]{:T(128)S(6)} %copy.166), kind=kOutput, calls=%fused_computation.34.clone.1 | convolution fusion | flops 330989568 | bytes 5348357 | tf_op jit(solution)/shard_map/while/body/eval_jaxpr/ol,cfl->ocf/dot_general | solution.py:55
  142.5 46.5 %while.79 = (s32[]{:T(128)}, f32[128,128,39]{1,0,2:T(8,128)S(1)}, f32[6,128,256]{1,2,0:T(8,128)}, f32[6,39,256]{2,1,0:T(8,128)}, bf16[6,128,256]{1,2,0:T(8,128)(...) while((s32[]{:T(128)}, f32[128,128,39]{1,0,2:T(8,128)S(1)}, ...), condition=%wide.region_17.18_spmd.clone, body=%wide.region_14.17_spmd.clone.sunk | while | flops 663257088 | bytes 13269675 | solution.py:66
  191.6 26.4 %while.80 = (s32[]{:T(128)}, f32[128,39,39]{0,2,1:T(8,128)}, f32[6,39,256]{2,1,0:T(8,128)}, f32[6,39,256]{2,1,0:T(8,128)}, bf16[6,128,256]{1,2,0:T(8,128)(2,1)S(...) while((s32[]{:T(128)}, f32[128,39,39]{0,2,1:T(8,128)}, ...), condition=%wide.region_21.22_spmd.clone, body=%wide.region_18.21_spmd.clone.sunk | while | flops 202076160 | bytes 2543487 | solution.py:66
  222.5 3.5 reshape.201
  228.5 3.4 reshape.202
  234.5 4.8 %all-to-all-start.2 = ((bf16[4,2,7680]{2,1,0:T(2,128)(2,1)}), bf16[4,2,7680]{2,1,0:T(2,128)(2,1)S(1)}, u32[]{:S(2)}, u32[]{:S(2)}) async-start(bf16[4,2,7680]{2,1,0:T(2,128)(2,1)} %reshape.241), calls=%async_computation.2 | async-start | bytes 245760 | tf_op jit(solution)/shard_map/all_to_all | solution.py:153
  239.3 3.5 all-to-all-done.2
  245.4 145.9 %all-reduce.3.cloned.1.call-done = (f32[128,1521]{0,1:T(8,128)}, f32[128,4992]{0,1:T(8,128)}, f32[128,4992]{0,1:T(8,128)}) async-done(((f32[128,1521]{0,1:T(8,128)}, f32[128,4992]{0,1:T(8,128)}, f32[128,4992]{0,1:T(8,128)}), (f32[128,1521]{0,1:T(8,128)}, f32[128,4992]{0,1:T(8,128)}, f32[128,4992]{0,1:T(8,128)})) %all-reduce.3.cloned.1.call-update) | async-done | bytes 5890576 | tf_op jit(solution)/shard_map/psum | solution.py:158
  393.6 5.4 %constant_dynamic-slice_fusion.2 = (f32[8,4992]{0,1:T(8,128)S(1)}, f32[8,4992]{0,1:T(8,128)}) fusion(f32[128,4992]{0,1:T(8,128)} %get-tuple-element.516, s32[]{:T(128)S(6)} %select_n.2, f32[128,4992]{0,1:T(8,128)} %get-tuple-element.515), kind=kLoop, calls=%fused_computation.132 | loop fusion | bytes 638980 | tf_op jit(solution)/shard_map/dynamic_slice | solution.py:162
  399.0 3.1 copy.99
  (289 shorter events, 159.2 us)
Async XLA Ops:
  8.1 1.8 copy-start.15
  8.1 7.4 %copy-start.14 = (bf16[3,128]{1,0:T(4,128)(2,1)S(1)}, bf16[3,128]{1,0:T(4,128)(2,1)}, u32[]{:S(2)}) copy-start(bf16[3,128]{1,0:T(4,128)(2,1)} %param.24) | copy-start | bytes 2308
  8.1 7.4 %copy-start.13 = (bf16[128,1521]{0,1:T(8,128)(2,1)S(1)}, bf16[128,1521]{0,1:T(8,128)(2,1)}, u32[]{:S(2)}) copy-start(bf16[128,1521]{0,1:T(8,128)(2,1)} %param.25) | copy-start | bytes 1168132
  8.1 8.3 %copy-start.4 = (bf16[128,4992]{1,0:T(8,128)(2,1)S(1)}, bf16[128,4992]{1,0:T(8,128)(2,1)}, u32[]{:S(2)}) copy-start(bf16[128,4992]{1,0:T(8,128)(2,1)} %param.26) | copy-start | bytes 3833860
  10.8 15.0 %all-to-all-start = ((bf16[4,2,7680]{2,1,0:T(2,128)(2,1)}), bf16[4,2,7680]{2,1,0:T(2,128)(2,1)S(1)}, u32[]{:S(2)}, u32[]{:S(2)}) async-start(bf16[4,2,7680]{2,1,0:T(2,128)(2,1)} %reshape.239), calls=%async_computation | async-start | bytes 245760 | tf_op jit(solution)/shard_map/all_to_all | solution.py:96
  18.0 3.6 copy-start.2
  18.0 2.1 copy-start.5
  21.6 4.4 %copy-start.17 = (s32[40]{0:T(128)S(1)}, s32[40]{0:T(128)}, u32[]{:S(2)}) copy-start(s32[40]{0:T(128)} %param.22) | copy-start | bytes 484
  23.9 2.8 copy-start.12
  64.8 7.1 %copy-start.3 = (bf16[6,128,256]{1,2,0:T(8,128)(2,1)}, bf16[6,128,256]{1,2,0:T(8,128)(2,1)S(1)}, u32[]{:S(2)}) copy-start(bf16[6,128,256]{1,2,0:T(8,128)(2,1)S(1)} %get-tuple-element.919) | copy-start | bytes 1179652
  65.6 9.5 %all-to-all-start.1 = ((f32[2,1,9216]{2,1,0:T(1,128)}), f32[2,1,9216]{2,1,0:T(1,128)S(1)}, u32[]{:S(2)}, u32[]{:S(2)}) async-start(f32[2,1,9216]{2,1,0:T(1,128)} %broadcast_in_dim.57), calls=%async_computation.1 | async-start | bytes 147456 | tf_op jit(solution)/shard_map/all_to_all | solution.py:15
  70.5 320.8 %all-reduce.3.cloned.1.call-start = ((), (), s32[]{:S(2)}) async-start(), calls=%async_computation.3 | async-start | bytes 11788288 | tf_op jit(solution)/shard_map/psum | solution.py:158
  70.6 4.9 %copy-start.19 = (s32[24]{0:T(128)S(1)}, s32[24]{0:T(128)}, u32[]{:S(2)}) copy-start(s32[24]{0:T(128)} %param.23) | copy-start | bytes 292
  79.8 3.4 copy-start.7
  89.1 4.4 %copy-start.7 = (bf16[128,128,39]{0,1,2:T(8,128)(2,1)S(1)}, bf16[128,128,39]{0,1,2:T(8,128)(2,1)}, u32[]{:S(2)}) copy-start(bf16[128,128,39]{0,1,2:T(8,128)(2,1)} %get-tuple-element.849) | copy-start | bytes 3833860 | tf_op jit(solution)/shard_map/while
  99.2 4.4 %copy-start.7 = (bf16[128,128,39]{0,1,2:T(8,128)(2,1)S(1)}, bf16[128,128,39]{0,1,2:T(8,128)(2,1)}, u32[]{:S(2)}) copy-start(bf16[128,128,39]{0,1,2:T(8,128)(2,1)} %get-tuple-element.849) | copy-start | bytes 3833860 | tf_op jit(solution)/shard_map/while
  109.4 4.4 %copy-start.7 = (bf16[128,128,39]{0,1,2:T(8,128)(2,1)S(1)}, bf16[128,128,39]{0,1,2:T(8,128)(2,1)}, u32[]{:S(2)}) copy-start(bf16[128,128,39]{0,1,2:T(8,128)(2,1)} %get-tuple-element.849) | copy-start | bytes 3833860 | tf_op jit(solution)/shard_map/while
  119.5 4.4 %copy-start.7 = (bf16[128,128,39]{0,1,2:T(8,128)(2,1)S(1)}, bf16[128,128,39]{0,1,2:T(8,128)(2,1)}, u32[]{:S(2)}) copy-start(bf16[128,128,39]{0,1,2:T(8,128)(2,1)} %get-tuple-element.849) | copy-start | bytes 3833860 | tf_op jit(solution)/shard_map/while
  129.7 4.4 %copy-start.7 = (bf16[128,128,39]{0,1,2:T(8,128)(2,1)S(1)}, bf16[128,128,39]{0,1,2:T(8,128)(2,1)}, u32[]{:S(2)}) copy-start(bf16[128,128,39]{0,1,2:T(8,128)(2,1)} %get-tuple-element.849) | copy-start | bytes 3833860 | tf_op jit(solution)/shard_map/while
  142.6 2.8 copy-start.6
  150.4 2.8 copy-start.6
  158.1 2.8 copy-start.6
  165.9 2.8 copy-start.6
  173.6 2.8 copy-start.6
  181.4 2.8 copy-start.6
  222.5 3.5 copy-start.1
  231.9 1.1 copy-start.9
  231.9 1.2 copy-start.10
  231.9 1.3 copy-start.11
  231.9 1.5 copy-start.18
  231.9 11.3 %copy-start.16 = (s32[1920]{0:T(1024)S(1)}, s32[1920]{0:T(1024)}, u32[]{:S(2)}) copy-start(s32[1920]{0:T(1024)} %copy-done.15) | copy-start | bytes 23044
  234.5 8.3 %all-to-all-start.2 = ((bf16[4,2,7680]{2,1,0:T(2,128)(2,1)}), bf16[4,2,7680]{2,1,0:T(2,128)(2,1)S(1)}, u32[]{:S(2)}, u32[]{:S(2)}) async-start(bf16[4,2,7680]{2,1,0:T(2,128)(2,1)} %reshape.241), calls=%async_computation.2 | async-start | bytes 245760 | tf_op jit(solution)/shard_map/all_to_all | solution.py:153
  (2 other events, 1.9 us)
Sparse Core Ops, SparseCore 0:
  232.0 159.2 all-reduce.2
where the time goes:
time: 413 us; the launch traced here: 410 us
  waiting for transfers between devices  150 us (36%)
  matrix products  136 us (33%)
  local copies, waits for them, and re-layouts  89 us (22%)
  starting transfers between devices  14.4 us (3%)
  between operations  14.3 us (3%)
  other arithmetic  5.7 us (1%)
    psum x1, waiting for transfers between devices, local(): summed = lax.psum((grad_one, grad_two, grad_three), ('dp', 'samp', 'col'))  146 us
    dot_general x18, matrix products, accumulate(): jnp.einsum('ol,cfl->ocf', cotangent_part, outer_products, preferred_eleme...  54.9 us
    dot_general x18, matrix products, accumulate(): jnp.einsum('ocf,ol->cfl', filter_cube, cotangent_part, preferred_element_...  39.5 us
    dot_general x18, matrix products, one_block(): jnp.einsum('ocf,cfl->ol', filter_cube, outer_products, preferred_element_...  36.7 us
    dynamic_update_slice x42, local copies, waits for them, and re-layouts, backward_layer(): lax.scan(accumulate, starting, (cotangent, previous, anchor))  31.2 us
    unnamed x47, local copies, waits for them, and re-layouts  15.8 us
    reshape x3, local copies, waits for them, and re-layouts, backward_layer(): running.reshape(filter_cube.shape[0], filter_cube.shape[1] * filter_cube....  8.99 us
  transfers between devices with their start and end apart: 4, of which 3 were waited for; matrix products, arithmetic and copies ran while one was open for 4% of the time, Pallas kernels for 0%

commit v1 on v0

v1 whole, which is shorter than its diff:
```python
import functools

import jax
import jax.numpy as jnp
from jax import lax
from jax.experimental import pallas as pl
from jax.experimental.pallas import tpu as pltpu
from jax.sharding import PartitionSpec as P

F = 39
FP = 40
H = 128
HALF = 20
PAIRS = 848
PL = 896
LANES = 1536
T2N = 12
BAGS = 512
SCALE = 16.0
BF = jnp.bfloat16
F32 = jnp.float32
VMEM = pl.BlockSpec(memory_space=pltpu.VMEM)
SMEM = pl.BlockSpec(memory_space=pltpu.SMEM)


def dot(a, b, ca, cb):
    return lax.dot_general(a, b, (((ca,), (cb,)), ((), ())), preferred_element_type=F32)


def lane_columns(row):
    n = row.shape[1] // 128
    blocks = [
        jnp.transpose(jnp.broadcast_to(row[:, b * 128 : (b + 1) * 128], (128, 128)))
        for b in range(n)
    ]
    return jnp.concatenate(blocks, axis=0)


def bag_places(ids):
    tens = (ids * 6554) >> 16
    twenties = (ids * 3277) >> 16
    row = twenties * 10 + (ids - tens * 10)
    row = row + 8 * ((row * 8739) >> 20)
    return row, tens - 2 * twenties


def pool(ids, rows):
    place, half = bag_places(ids)
    half_col = lane_columns(half.astype(F32))
    lane = lax.broadcasted_iota(jnp.int32, half_col.shape, 1)
    keep = half_col == (lane >= 64).astype(F32)
    wide = jnp.concatenate([rows, rows], axis=1)
    wide = jnp.where(keep, wide.astype(F32), 0.0).astype(BF)
    n = ids.shape[1]
    spot = lax.broadcasted_iota(jnp.int32, (BAGS, n), 0)
    member = jnp.where(jnp.broadcast_to(place, (BAGS, n)) == spot, 1.0, 0.0).astype(BF)
    return dot(member, wide, 1, 0).astype(BF)


def slot_row(slots):
    owner = (slots * 6554) >> 16
    base = owner * 128 + (slots - owner * 10)
    parts = [base + 10 * t for t in range(T2N)]
    parts.append(jnp.full((1, 512 - FP * T2N), -1, jnp.int32))
    return jnp.concatenate(parts, axis=1)


def gather_fields(slots, arrived):
    col = lane_columns(slot_row(slots).astype(F32))[: FP * T2N]
    parts = []
    for b in range(BAGS // 128):
        lane = lax.broadcasted_iota(jnp.int32, col.shape, 1) + 128 * b
        parts.append(jnp.where(col == lane.astype(F32), 1.0, 0.0).astype(BF))
    chooser = jnp.concatenate(parts, axis=1)
    picked = dot(chooser, arrived, 1, 0)
    x = jnp.concatenate([picked[FP * t : FP * (t + 1)] for t in range(T2N)], axis=1)
    field = lax.broadcasted_iota(jnp.int32, x.shape, 0)
    return jnp.where(field == F, 1.0, x)


def scatter_fields(slots, grads):
    row = slot_row(slots)
    spot = lax.broadcasted_iota(jnp.int32, (BAGS, 512), 0)
    member = jnp.where(jnp.broadcast_to(row, (BAGS, 512)) == spot, 1.0, 0.0).astype(BF)
    tall = [grads[:, 128 * t : 128 * (t + 1)] for t in range(T2N)]
    tall.append(jnp.zeros((512 - FP * T2N, 128), F32))
    tall = jnp.concatenate(tall, axis=0).astype(BF)
    return dot(member, tall, 1, 0).astype(BF)


def spread_rows(ids, returned):
    place, half = bag_places(ids)
    place_col = lane_columns(place.astype(F32))
    half_col = lane_columns(half.astype(F32))
    parts = []
    for b in range(BAGS // 128):
        lane = lax.broadcasted_iota(jnp.int32, place_col.shape, 1) + 128 * b
        parts.append(jnp.where(place_col == lane.astype(F32), 1.0, 0.0).astype(BF))
    member = jnp.concatenate(parts, axis=1)
    both = dot(member, returned, 1, 0)
    return jnp.where(half_col[:, :64] == 0.0, both[:, :64], both[:, 64:]).astype(BF)


def pairs_from(full, k, stride, out, zero_tail=True):
    step = stride + 1
    low = full[pl.ds(k, F - k, stride=step), :]
    if k:
        low = low + full[pl.ds(k * stride, F - k, stride=step), :]
    out[pl.ds(FP * k, F - k), :] = low
    if k:
        high = full[pl.ds((F - k) * stride, k, stride=step), :]
        high = high + full[pl.ds(F - k, k, stride=step), :]
        out[pl.ds(FP * k + F - k, k), :] = high


def pairs_to(src, first, k, stride, full):
    step = stride + 1
    low = src[pl.ds(first + FP * k, F - k), :]
    full[pl.ds(k, F - k, stride=step), :] = low
    if k:
        full[pl.ds(k * stride, F - k, stride=step), :] = low
        high = src[pl.ds(first + FP * k + F - k, k), :]
        full[pl.ds((F - k) * stride, k, stride=step), :] = high
        full[pl.ds(F - k, k, stride=step), :] = high


def prepare(w1_ref, w2_ref, w3_ref, out_w, tall, full, sym_q, sym_w, u_ref, a_ref, at_ref):
    lane = lax.broadcasted_iota(jnp.int32, (H, 128), 1)
    sublane = lax.broadcasted_iota(jnp.int32, (H, 128), 0)
    w3_col = lane_columns(out_w[2:3, :]).astype(BF)
    tall[...] = dot(w3_ref[...], w3_col, 0, 0)
    u = jnp.where(lane == F, lane_columns(out_w[1:2, :]), 0.0)
    for i in range(F):
        u = jnp.where(lane == i, tall[pl.ds(i, H, stride=F), :], u)
    u = u.astype(BF)
    u_ref[...] = u
    eye = jnp.where(lane == sublane, 1.0, 0.0).astype(BF)
    full[pl.ds(0, F * F), :] = dot(w1_ref[...], eye, 0, 0)
    sym_w[...] = jnp.zeros_like(sym_w)
    for k in range(HALF):
        pairs_from(full, k, F, sym_w)
    tall[...] = dot(w2_ref[...], u, 0, 0)
    for i in range(F):
        block = jnp.transpose(tall[pl.ds(i, H, stride=F), :])
        full[pl.ds(FP * i, FP), :] = block[:FP]
    sym_q[...] = jnp.zeros_like(sym_q)
    for k in range(HALF):
        pairs_from(full, k, FP, sym_q)
    sym_q[pl.ds(FP * HALF, F), :] = full[pl.ds(F, F, stride=FP), :]
    sym_q[pl.ds(FP * HALF + F, 1), :] = out_w[0:1, :]
    a_ref[:, :H] = sym_q[:PAIRS].astype(BF)
    a_ref[:, H:] = sym_w[:PAIRS].astype(BF)
    for b in range(PL // 128):
        at_ref[:H, 128 * b : 128 * (b + 1)] = jnp.transpose(sym_w[128 * b : 128 * (b + 1)]).astype(BF)
        at_ref[H:, 128 * b : 128 * (b + 1)] = jnp.transpose(sym_q[128 * b : 128 * (b + 1)]).astype(BF)


def forward(x, at_ref, xx, z_ref, y_ref):
    xx[0:FP, :] = x
    xx[F : F + FP, :] = x
    ones = xx[0:FP, :]
    field = lax.broadcasted_iota(jnp.int32, (FP, LANES), 0)
    x1 = jnp.where(field == F, 1.0, ones)
    for b in range(HALF // 2):
        two = [x1 * xx[pl.ds(k, FP), :] for k in (2 * b, 2 * b + 1)]
        z_ref[pl.ds(2 * FP * b, 2 * FP), :] = jnp.concatenate(two, axis=0).astype(BF)
    z_ref[pl.ds(FP * HALF, PL - FP * HALF), :] = jnp.concatenate(
        [x1, jnp.zeros((PL - FP * HALF - FP, LANES), F32)], axis=0
    ).astype(BF)
    y_ref[...] = dot(at_ref[...], z_ref[...], 1, 0)
    total = jnp.sum(y_ref[:H, :] * y_ref[H:, :], axis=0, keepdims=True)
    total = jnp.concatenate([total[:, 128 * t : 128 * (t + 1)] for t in range(T2N)], axis=0)
    first = lax.broadcasted_iota(jnp.int32, total.shape, 1) < 64
    low = jnp.sum(jnp.where(first, total, 0.0), axis=1, keepdims=True)
    high = jnp.sum(jnp.where(first, 0.0, total), axis=1, keepdims=True)
    return jnp.where(first, low, high)


def slope_row(logits, labels_ref):
    row = lax.broadcasted_iota(jnp.int32, (T2N, 128), 0)
    lane = lax.broadcasted_iota(jnp.int32, (T2N, 128), 1)
    sample = 2 * row + (lane >= 64).astype(jnp.int32)
    labels = jnp.zeros((T2N, 128), F32)
    for n in range(2 * T2N):
        labels = jnp.where(sample == n, labels_ref[n].astype(F32), labels)
    slope = SCALE * (1.0 / (1.0 + jnp.exp(-logits)) - labels)
    return jnp.concatenate([slope[t : t + 1] for t in range(T2N)], axis=1)


def weight_sums(slope, y_ref, z_ref, sy_ref):
    sy_ref[...] = (y_ref[...] * slope).astype(BF)
    both = dot(z_ref[:PAIRS], sy_ref[...], 1, 1)
    return jnp.concatenate([both[:, :H], both[:, H:]], axis=0)


def field_grads(a_ref, sy_ref, xx, acc):
    r = dot(a_ref[...], sy_ref[...], 1, 0)
    field = lax.broadcasted_iota(jnp.int32, (FP, LANES), 0)
    acc[...] = jnp.zeros_like(acc)
    total = r[FP * HALF : FP * HALF + FP]
    x = xx[0:FP, :]
    for k in range(HALF):
        block = r[FP * k : FP * (k + 1)]
        total = total + block * xx[pl.ds(k, FP), :]
        acc[pl.ds(k, FP), :] += block * x
    total = total + acc[0:FP, :] + acc[F : F + FP, :]
    return jnp.where(field == F, 0.0, total)


def finish(sums, u_mine, w3_mine, mine, w2_ref, full, tall, g1_ref, g2_ref, g3_ref):
    lane = lax.broadcasted_iota(jnp.int32, (H, 128), 1)
    for k in range(HALF):
        pairs_to(sums, PAIRS, k, F, full)
    rows = full[pl.ds(0, F * F), :].astype(BF)
    g1_ref[...] = dot(mine, rows, 1, 1)
    for k in range(HALF):
        pairs_to(sums, 0, k, FP, full)
    full[pl.ds(F, F, stride=FP), :] = sums[pl.ds(FP * HALF, F), :]
    for i in range(F):
        block = jnp.concatenate([full[pl.ds(FP * i, FP), :], jnp.zeros((128 - FP, 128), F32)], axis=0)
        tall[pl.ds(i, H, stride=F), :] = jnp.transpose(block)
    flat = tall[...].astype(BF)
    g2_ref[...] = dot(u_mine, flat, 1, 1)
    v3 = dot(w2_ref[...], flat, 1, 0)
    for i in range(F):
        tall[pl.ds(i, H, stride=F), :] = jnp.where(lane == i, v3, 0.0)
    g3_ref[...] = dot(w3_mine, tall[...].astype(BF), 1, 1)


def params(**kw):
    return pltpu.CompilerParams(vmem_limit_bytes=60 << 20, **kw)


def k_pool(ids_ref, rows_ref, out_ref):
    out_ref[...] = pool(ids_ref[...], rows_ref[0])


def k_prep(w1_ref, w2_ref, w3_ref, ow_ref, u_ref, a_ref, at_ref, tall, full, sym_q, sym_w):
    prepare(w1_ref, w2_ref, w3_ref, ow_ref[...].astype(F32), tall, full, sym_q, sym_w, u_ref, a_ref, at_ref)


def k_forward(slots_ref, arrived_ref, at_ref, xx, z_ref, y_ref, sums_ref):
    x = gather_fields(slots_ref[...], arrived_ref[...])
    sums_ref[...] = forward(x, at_ref, xx, z_ref, y_ref)


def k_backward(labels_ref, slots_ref, logits_ref, xx, z_ref, y_ref, a_ref, sums_ref, out_ref, sy_ref, acc):
    slope = slope_row(logits_ref[...], labels_ref)
    sums_ref[...] = weight_sums(slope, y_ref, z_ref, sy_ref)
    out_ref[...] = scatter_fields(slots_ref[...], field_grads(a_ref, sy_ref, xx, acc))


def k_rows(ids_ref, returned_ref, out_ref):
    out_ref[0] = spread_rows(ids_ref[...], returned_ref[...])


def k_finish(sums_ref, u_ref, ow_ref, w2_ref, g1_ref, g2_ref, g3_ref, full, tall):
    dp = lax.axis_index("dp")
    row = lax.broadcasted_iota(jnp.int32, (8, 128), 0)
    lane = lax.broadcasted_iota(jnp.int32, (8, 128), 1)
    mine = jnp.where(lane == row + 8 * dp, 1.0, 0.0).astype(BF)
    u_mine = dot(mine, u_ref[...], 1, 0).astype(BF)
    w3 = jnp.broadcast_to(ow_ref[2:3, :].astype(F32), (8, 128))
    w3 = jnp.sum(jnp.where(lane == row + 8 * dp, w3, 0.0), axis=1, keepdims=True)
    w3_mine = jnp.broadcast_to(w3, (8, 128)).astype(BF)
    finish(sums_ref, u_mine, w3_mine, mine, w2_ref, full, tall, g1_ref, g2_ref, g3_ref)


def shape(dims, dtype):
    return jax.ShapeDtypeStruct(dims, dtype)


TALL = pltpu.VMEM((F * H, 128), F32)
FULL = pltpu.VMEM((F * FP, 128), F32)


def call(kernel, outs, specs, scratch=()):
    single = not isinstance(outs, (tuple, list))
    return pl.pallas_call(
        kernel,
        out_shape=outs,
        in_specs=specs,
        out_specs=VMEM if single else [VMEM] * len(outs),
        scratch_shapes=scratch,
        compiler_params=params(),
    )


def run_pool(ids, rows):
    return call(k_pool, shape((BAGS, 128), BF), [VMEM] * 2)(ids, rows)


def run_prep(w1, w2, w3, ow):
    sym = pltpu.VMEM((PL, 128), F32)
    outs = [shape((H, 128), BF), shape((PAIRS, 256), BF), shape((256, PL), BF)]
    return call(k_prep, outs, [VMEM] * 4, [TALL, FULL, sym, sym])(w1, w2, w3, ow)


def run_forward(slots, arrived, at):
    outs = [shape((88, LANES), F32), shape((PL, LANES), BF), shape((256, LANES), F32), shape((T2N, 128), F32)]
    return call(k_forward, outs, [VMEM] * 3)(slots, arrived, at)


def run_backward(labels, slots, logits, xx, z, y, a):
    outs = [shape((2 * PAIRS, 128), F32), shape((BAGS, 128), BF)]
    scratch = [pltpu.VMEM((256, LANES), BF), pltpu.VMEM((88, LANES), F32)]
    return call(k_backward, outs, [SMEM] + [VMEM] * 6, scratch)(labels, slots, logits, xx, z, y, a)


def run_rows(ids, returned):
    return call(k_rows, shape((1, ids.shape[1], 64), BF), [VMEM] * 2)(ids, returned)


def run_finish(sums, u, ow, w2):
    outs = [shape((8, F * F), F32), shape((8, F * H), F32), shape((8, F * H), F32)]
    return call(k_finish, outs, [VMEM] * 4, [FULL, TALL])(sums, u, ow, w2)


def local(looked_rows, bag_ids, slot_of, labels, out_weight, filter_first, filter_second, filter_third):
    slots = slot_of.reshape(1, FP)
    pooled = run_pool(bag_ids, looked_rows)
    arrived = lax.all_to_all(pooled, "samp", 0, 0, tiled=True)
    u, a, at = run_prep(filter_first, filter_second, filter_third, out_weight)
    xx, z, y, sums = run_forward(slots, arrived, at)
    logits = sums + lax.ppermute(sums, "col", [(0, 1), (1, 0)])
    weight, slot_grads = run_backward(labels, slots, logits, xx, z, y, a)
    weight = lax.psum(weight, ("dp", "samp", "col"))
    returned = lax.all_to_all(slot_grads, "samp", 0, 0, tiled=True)
    row_grads = run_rows(bag_ids, returned)
    return (row_grads, *run_finish(weight, u, out_weight, filter_second))


def solution(mesh):
    in_specs = (
        P(("dp", "samp"), None, "col"),
        P(("dp", "samp"), None),
        P(),
        P(("dp", "samp")),
        P(),
        P(),
        P(),
        P(),
    )
    out_specs = (P(("dp", "samp"), None, "col"), P("dp", None), P("dp", None), P("dp", None))
    return jax.shard_map(local, mesh=mesh, in_specs=in_specs, out_specs=out_specs, check_vma=False)
```

time: 413 us -> 201 us (0.49)
  matrix products: 136 us -> 0 us
  local copies, waits for them, and re-layouts: 89 us -> 5.53 us
  Pallas kernels: 0 us -> 25 us
  waiting for transfers between devices: 150 us -> 137 us
  blocking collectives: 0 us -> 8.58 us
  starting transfers between devices: 14.4 us -> 8.41 us
  other arithmetic: 5.7 us -> 1.3 us
    dot_general x61 -> x0, matrix products: 136 us -> none  [the longest x18 54.9 us: accumulate(): jnp.einsum('ol,cfl->ocf', cotangent_part, outer_products, preferred_eleme...]
    dynamic_update_slice x42 -> x0, local copies, waits for them, and re-layouts: 31.2 us -> none  [backward_layer(): lax.scan(accumulate, starting, (cotangent, previous, anchor))]
    pallas_call x0 -> x6, Pallas kernels: none -> 25 us  [the longest x1 5.74 us: run_backward(): call(k_backward, outs, [SMEM] + [VMEM] * 6, scratch)]
    reshape x11 -> x0, local copies, waits for them, and re-layouts: 13.2 us -> none  [the longest x3 8.99 us: backward_layer(): running.reshape(filter_cube.shape[0], filter_cube.shape[1] * filter_cube....]
    dynamic_slice x26 -> x0, local copies, waits for them, and re-layouts: 13.1 us -> none  [the longest x2 6.76 us: local(): lax.dynamic_slice_in_dim(member_sum, offset, share_rows, 0)]
    unnamed x47 -> x7, local copies, waits for them, and re-layouts: 15.8 us -> 5.53 us
    psum x1, waiting for transfers between devices: 146 us -> 136 us  [local(): weight = lax.psum(weight, ('dp', 'samp', 'col'))]
    all_to_all x3 -> x1, starting transfers between devices: 14.4 us -> 4.72 us  [local(): arrived = lax.all_to_all(pooled, 'samp', 0, 0, tiled=True)]
  transfers between devices with their start and end apart: 4 -> 3, of which waited for: 3 -> 2; matrix products, arithmetic and copies ran while one was open for 4% -> 1% of each run, Pallas kernels for 0% -> 4%
where the time goes in v1:
time: 201 us; the launch traced here: 200 us
  waiting for transfers between devices  137 us (68%)
  Pallas kernels  25 us (12%)
  between operations  14 us (7%)
  blocking collectives  8.58 us (4%)
  starting transfers between devices  8.41 us (4%)
  local copies, waits for them, and re-layouts  5.53 us (3%)
    psum x1, waiting for transfers between devices, local(): weight = lax.psum(weight, ('dp', 'samp', 'col'))  136 us
    all_to_all x1, blocking collectives, local(): returned = lax.all_to_all(slot_grads, 'samp', 0, 0, tiled=True)  8.58 us
    pallas_call x1, Pallas kernels, run_backward(): call(k_backward, outs, [SMEM] + [VMEM] * 6, scratch)  5.74 us
    unnamed x7, local copies, waits for them, and re-layouts  5.53 us
    pallas_call x1, Pallas kernels, run_prep(): call(k_prep, outs, [VMEM] * 4, [TALL, FULL, sym, sym])(w1, w2, w3, ow)  5.36 us
    all_to_all x1, starting transfers between devices, local(): arrived = lax.all_to_all(pooled, 'samp', 0, 0, tiled=True)  4.72 us
    pallas_call x1, Pallas kernels, run_finish(): return call(k_finish, outs, [VMEM] * 4, [FULL, TALL])(sums, u, ow, w2)  4.49 us
    pallas_call x1, Pallas kernels, run_forward(): return call(k_forward, outs, [VMEM] * 3)(slots, arrived, at)  4.28 us
  transfers between devices with their start and end apart: 3, of which 2 were waited for; matrix products, arithmetic and copies ran while one was open for 1% of the time, Pallas kernels for 4%

profile of v1, /device:TPU:1, one launch (start us, length us, event | category | flops | bytes accessed | tf_op | source)
XLA Modules:
  0.0 200.3 jit_solution(7461649067245274746)
XLA Ops:
  7.2 0.0 copy-start.1
  7.2 2.0 copy.12.rows_ref
  9.2 2.6 %shard_map.111 = bf16[512,128]{1,0:T(8,128)(2,1)} custom-call(s32[1,1920]{1,0:T(1,128)} %ids_ref.3, bf16[1,1920,64]{2,1,0:T(8,128)(2,1)} %copy.12.rows_ref), custom_call_target="tpu_custom_call" | custom-call | tf_op jit(solution)/shard_map/pallas_call | solution.py:290
  11.7 4.7 %all-to-all-start = ((bf16[4,128,128]{2,1,0:T(8,128)(2,1)}), bf16[4,128,128]{2,1,0:T(8,128)(2,1)S(1)}, u32[]{:S(2)}, u32[]{:S(2)}) async-start(bf16[4,128,128]{2,1,0:T(8,128)(2,1)} %bitcast.6), calls=%async_computation | async-start | bytes 262144 | tf_op jit(solution)/shard_map/all_to_all | solution.py:322
  16.4 0.0 all-reduce.2.cloned.1.call-start
  16.4 0.0 copy-done.1
  16.4 1.0 copy.13.w1_ref
  17.4 5.4 %shard_map.112 = (bf16[128,128]{1,0:T(8,128)(2,1)}, bf16[848,256]{1,0:T(8,128)(2,1)}, bf16[256,896]{1,0:T(8,128)(2,1)}) custom-call(bf16[128,1521]{1,0:T(8,128)(2,1)} %copy.13.w1_ref, bf16[128,4992]{1,0:T(8,128)(2,1)} %w2_ref.3, bf16[128,4992]{1,0:T(8,128)(2,1)} %w3_ref.1, bf16[3,128]{1,0:T(4,128)(2,1)} %ow_ref.3), custom_call_target="tpu_custom_call" | custom-call | tf_op jit(solution)/shard_map/pallas_call | solution.py:296
  22.8 0.0 all-to-all-done
  22.8 0.0 copy-start
  22.8 0.7 copy-done
  23.4 4.3 %shard_map.113 = (f32[88,1536]{1,0:T(8,128)}, bf16[896,1536]{1,0:T(8,128)(2,1)}, f32[256,1536]{1,0:T(8,128)}, f32[12,128]{1,0:T(8,128)}) custom-call(s32[1,40]{1,0:T(1,128)} %bitcast.9, bf16[512,128]{1,0:T(8,128)(2,1)} %bitcast.5, bf16[256,896]{1,0:T(8,128)(2,1)} %get-tuple-element.16.at_ref), custom_call_target="tpu_custom_call" | custom-call | tf_op jit(solution)/shard_map/pallas_call | solution.py:301
  27.7 3.7 %collective-permute-start = (f32[12,128]{1,0:T(8,128)}, f32[12,128]{1,0:T(8,128)S(1)}, u32[]{:S(2)}, u32[]{:S(2)}) collective-permute-start(f32[12,128]{1,0:T(8,128)} %get-tuple-element.17), channel_id=1, source_target_pairs={{0,1},{1,0},{2,3},{3,2},{4,5},{5,4},{6,7},{7,6},{8,9},{9,8},{10,11... | collective-permute-start | bytes 18440 | tf_op jit(solution)/shard_map/ppermute | solution.py:325
  31.4 1.2 collective-permute-done
  32.6 1.3 add.5.logits_ref
  33.9 5.7 %shard_map.114 = (f32[1696,128]{1,0:T(8,128)}, bf16[512,128]{1,0:T(8,128)(2,1)}) custom-call(s32[24]{0:T(128)} %labels_ref.1, s32[1,40]{1,0:T(1,128)} %bitcast.10, f32[12,128]{1,0:T(8,128)} %add.5.logits_ref, f32[88,1536]{1,0:T(8,128)} %get-tuple-element.18.xx, bf16[896,1536]{1,0:T(8,128)(2,1)} %get-tuple-element.19.z_ref, ...), custom_call_target="tpu_custom_call" | custom-call | tf_op jit(solution)/shard_map/pallas_call | solution.py:307
  39.7 0.0 all-reduce.2.cloned.1.call-update
  39.7 8.6 %all_to_all.22 = bf16[4,128,128]{2,1,0:T(8,128)(2,1)} all-to-all(bf16[4,128,128]{2,1,0:T(8,128)(2,1)} %bitcast.8), channel_id=1, replica_groups=mesh['dp'=16,'samp'=4,'col'=2] {'samp'}, dimensions={0} | all-to-all | bytes 262144 | tf_op jit(solution)/shard_map/all_to_all | solution.py:328
  48.3 2.6 %shard_map.115 = bf16[1,1920,64]{2,1,0:T(8,128)(2,1)} custom-call(s32[1,1920]{1,0:T(1,128)} %ids_ref.3, bf16[512,128]{1,0:T(8,128)(2,1)} %bitcast.7), custom_call_target="tpu_custom_call" | custom-call | tf_op jit(solution)/shard_map/pallas_call | solution.py:311
  50.8 1.9 copy.14
  52.8 136.2 %all-reduce.2.cloned.1.call-done.sums_ref = f32[1696,128]{1,0:T(8,128)} async-done(((f32[1696,128]{1,0:T(8,128)}), f32[1696,128]{1,0:T(8,128)}) %all-reduce.2.cloned.1.call-update) | async-done | bytes 868368 | tf_op jit(solution)/shard_map/psum | solution.py:327
  188.9 4.5 %shard_map.116 = (f32[8,1521]{1,0:T(8,128)}, f32[8,4992]{1,0:T(8,128)}, f32[8,4992]{1,0:T(8,128)}) custom-call(f32[1696,128]{1,0:T(8,128)} %all-reduce.2.cloned.1.call-done.sums_ref, bf16[128,128]{1,0:T(8,128)(2,1)} %get-tuple-element.24.u_ref, bf16[3,128]{1,0:T(4,128)(2,1)} %ow_ref.3, bf16[128,4992]{1,0:T(8,128)(2,1)} %w2_ref.3), custom_call_target="tpu_custom_call" | custom-call | tf_op jit(solution)/shard_map/pallas_call | solution.py:316
Async XLA Ops:
  7.2 9.3 %copy-start.1 = (bf16[128,1521]{0,1:T(8,128)(2,1)S(1)}, bf16[128,1521]{0,1:T(8,128)(2,1)}, u32[]{:S(2)}) copy-start(bf16[128,1521]{0,1:T(8,128)(2,1)} %param.13) | copy-start | bytes 1168132
  11.7 11.1 %all-to-all-start = ((bf16[4,128,128]{2,1,0:T(8,128)(2,1)}), bf16[4,128,128]{2,1,0:T(8,128)(2,1)S(1)}, u32[]{:S(2)}, u32[]{:S(2)}) async-start(bf16[4,128,128]{2,1,0:T(8,128)(2,1)} %bitcast.6), calls=%async_computation | async-start | bytes 262144 | tf_op jit(solution)/shard_map/all_to_all | solution.py:322
  16.4 172.5 %all-reduce.2.cloned.1.call-start = ((), (), s32[]{:S(2)}) async-start(), calls=%async_computation.2 | async-start | bytes 1736704 | tf_op jit(solution)/shard_map/psum | solution.py:327
  22.8 0.7 copy-start
  27.7 4.9 %collective-permute-start = (f32[12,128]{1,0:T(8,128)}, f32[12,128]{1,0:T(8,128)S(1)}, u32[]{:S(2)}, u32[]{:S(2)}) collective-permute-start(f32[12,128]{1,0:T(8,128)} %get-tuple-element.17), channel_id=1, source_target_pairs={{0,1},{1,0},{2,3},{3,2},{4,5},{5,4},{6,7},{7,6},{8,9},{9,8},{10,11... | collective-permute-start | bytes 18440 | tf_op jit(solution)/shard_map/ppermute | solution.py:325
Sparse Core Ops, SparseCore 0:
  39.8 149.0 all-reduce.1

commit v2 on v1

v2 whole, which is shorter than its diff:
```python
import functools

import jax
import jax.numpy as jnp
from jax import lax
from jax.experimental import pallas as pl
from jax.experimental.pallas import tpu as pltpu
from jax.sharding import PartitionSpec as P

F = 39
FP = 40
H = 128
HALF = 20
PAIRS = 848
PL = 896
LANES = 1536
T2N = 12
BAGS = 512
SCALE = 16.0
BF = jnp.bfloat16
F32 = jnp.float32
VMEM = pl.BlockSpec(memory_space=pltpu.VMEM)
SMEM = pl.BlockSpec(memory_space=pltpu.SMEM)


def dot(a, b, ca, cb):
    return lax.dot_general(a, b, (((ca,), (cb,)), ((), ())), preferred_element_type=F32)


def lane_columns(row):
    n = row.shape[1] // 128
    blocks = [
        jnp.transpose(jnp.broadcast_to(row[:, b * 128 : (b + 1) * 128], (128, 128)))
        for b in range(n)
    ]
    return jnp.concatenate(blocks, axis=0)


def bag_places(ids):
    tens = (ids * 6554) >> 16
    twenties = (ids * 3277) >> 16
    row = twenties * 10 + (ids - tens * 10)
    row = row + 8 * ((row * 8739) >> 20)
    return row, tens - 2 * twenties


def bag_member(ids):
    place, _ = bag_places(ids)
    n = ids.shape[1]
    spot = lax.broadcasted_iota(jnp.int32, (BAGS, n), 0)
    return jnp.where(jnp.broadcast_to(place, (BAGS, n)) == spot, 1.0, 0.0).astype(BF)


def pool(ids, rows, member):
    half = bag_places(ids)[1].astype(F32)
    rows = rows.astype(F32)
    wide = jnp.concatenate([rows * (1.0 - half), rows * half], axis=0).astype(BF)
    return dot(member, wide, 1, 1).astype(BF)


def slot_row(slots):
    owner = (slots * 6554) >> 16
    base = owner * 128 + (slots - owner * 10)
    parts = [base + 10 * t for t in range(T2N)]
    parts.append(jnp.full((1, 512 - FP * T2N), -1, jnp.int32))
    return jnp.concatenate(parts, axis=1)


def gather_fields(slots, arrived):
    col = lane_columns(slot_row(slots).astype(F32))[: FP * T2N]
    parts = []
    for b in range(BAGS // 128):
        lane = lax.broadcasted_iota(jnp.int32, col.shape, 1) + 128 * b
        parts.append(jnp.where(col == lane.astype(F32), 1.0, 0.0).astype(BF))
    chooser = jnp.concatenate(parts, axis=1)
    picked = dot(chooser, arrived, 1, 0)
    x = jnp.concatenate([picked[FP * t : FP * (t + 1)] for t in range(T2N)], axis=1)
    field = lax.broadcasted_iota(jnp.int32, x.shape, 0)
    return jnp.where(field == F, 1.0, x)


def scatter_fields(slots, grads):
    row = slot_row(slots)
    spot = lax.broadcasted_iota(jnp.int32, (BAGS, 512), 0)
    member = jnp.where(jnp.broadcast_to(row, (BAGS, 512)) == spot, 1.0, 0.0).astype(BF)
    tall = [grads[:, 128 * t : 128 * (t + 1)] for t in range(T2N)]
    tall.append(jnp.zeros((512 - FP * T2N, 128), F32))
    tall = jnp.concatenate(tall, axis=0).astype(BF)
    return dot(member, tall, 1, 0).astype(BF)


def spread_rows(ids, member, returned):
    half = bag_places(ids)[1]
    both = dot(returned, member, 0, 0)
    return jnp.where(half == 0, both[:64], both[64:]).astype(BF)


def pairs_from(full, k, stride, out, zero_tail=True):
    step = stride + 1
    low = full[pl.ds(k, F - k, stride=step), :]
    if k:
        low = low + full[pl.ds(k * stride, F - k, stride=step), :]
    out[pl.ds(FP * k, F - k), :] = low
    if k:
        high = full[pl.ds((F - k) * stride, k, stride=step), :]
        high = high + full[pl.ds(F - k, k, stride=step), :]
        out[pl.ds(FP * k + F - k, k), :] = high


def pairs_to(src, first, k, stride, full):
    step = stride + 1
    low = src[pl.ds(first + FP * k, F - k), :]
    full[pl.ds(k, F - k, stride=step), :] = low
    if k:
        full[pl.ds(k * stride, F - k, stride=step), :] = low
        high = src[pl.ds(first + FP * k + F - k, k), :]
        full[pl.ds((F - k) * stride, k, stride=step), :] = high
        full[pl.ds(F - k, k, stride=step), :] = high


def prepare(w1_ref, w2_ref, w3_ref, out_w, tall, full, sym_q, sym_w, u_ref, a_ref, at_ref):
    lane = lax.broadcasted_iota(jnp.int32, (H, 128), 1)
    w3_col = lane_columns(out_w[2:3, :]).astype(BF)
    tall[...] = dot(w3_ref[...], w3_col, 0, 0)
    u = jnp.where(lane == F, lane_columns(out_w[1:2, :]), 0.0)
    for i in range(F):
        u = jnp.where(lane == i, tall[pl.ds(i, H, stride=F), :], u)
    u = u.astype(BF)
    u_ref[...] = u
    full[pl.ds(0, F * F), :] = w1_ref[...].astype(F32)
    sym_w[...] = jnp.zeros_like(sym_w)
    for k in range(HALF):
        pairs_from(full, k, F, sym_w)
    tall[...] = dot(w2_ref[...], u, 0, 0)
    for i in range(F):
        block = jnp.transpose(tall[pl.ds(i, H, stride=F), :])
        full[pl.ds(FP * i, FP), :] = block[:FP]
    sym_q[...] = jnp.zeros_like(sym_q)
    for k in range(HALF):
        pairs_from(full, k, FP, sym_q)
    sym_q[pl.ds(FP * HALF, F), :] = full[pl.ds(F, F, stride=FP), :]
    sym_q[pl.ds(FP * HALF + F, 1), :] = out_w[0:1, :]
    a_ref[:, :H] = sym_w[:PAIRS].astype(BF)
    a_ref[:, H:] = sym_q[:PAIRS].astype(BF)
    for b in range(PL // 128):
        at_ref[:H, 128 * b : 128 * (b + 1)] = jnp.transpose(sym_w[128 * b : 128 * (b + 1)]).astype(BF)
        at_ref[H:, 128 * b : 128 * (b + 1)] = jnp.transpose(sym_q[128 * b : 128 * (b + 1)]).astype(BF)


def forward(x, at_ref, xx, z_ref, y_ref):
    xx[0:FP, :] = x
    xx[F : F + FP, :] = x
    ones = xx[0:FP, :]
    field = lax.broadcasted_iota(jnp.int32, (FP, LANES), 0)
    x1 = jnp.where(field == F, 1.0, ones)
    for b in range(HALF // 2):
        two = [x1 * xx[pl.ds(k, FP), :] for k in (2 * b, 2 * b + 1)]
        z_ref[pl.ds(2 * FP * b, 2 * FP), :] = jnp.concatenate(two, axis=0).astype(BF)
    z_ref[pl.ds(FP * HALF, PL - FP * HALF), :] = jnp.concatenate(
        [x1, jnp.zeros((PL - FP * HALF - FP, LANES), F32)], axis=0
    ).astype(BF)
    y_ref[...] = dot(at_ref[...], z_ref[...], 1, 0)
    total = jnp.sum(y_ref[:H, :] * y_ref[H:, :], axis=0, keepdims=True)
    total = jnp.concatenate([total[:, 128 * t : 128 * (t + 1)] for t in range(T2N)], axis=0)
    first = lax.broadcasted_iota(jnp.int32, total.shape, 1) < 64
    low = jnp.sum(jnp.where(first, total, 0.0), axis=1, keepdims=True)
    high = jnp.sum(jnp.where(first, 0.0, total), axis=1, keepdims=True)
    return jnp.where(first, low, high)


def slope_row(logits, labels_ref):
    row = lax.broadcasted_iota(jnp.int32, (T2N, 128), 0)
    lane = lax.broadcasted_iota(jnp.int32, (T2N, 128), 1)
    sample = 2 * row + (lane >= 64).astype(jnp.int32)
    labels = jnp.zeros((T2N, 128), F32)
    for n in range(2 * T2N):
        labels = jnp.where(sample == n, labels_ref[n].astype(F32), labels)
    slope = SCALE * (1.0 / (1.0 + jnp.exp(-logits)) - labels)
    return jnp.concatenate([slope[t : t + 1] for t in range(T2N)], axis=1)


def field_grads(a_ref, y16, xx, acc):
    swapped = jnp.concatenate([y16[H:], y16[:H]], axis=0)
    r = dot(a_ref[...], swapped, 1, 0)
    field = lax.broadcasted_iota(jnp.int32, (FP, LANES), 0)
    acc[...] = jnp.zeros_like(acc)
    total = r[FP * HALF : FP * HALF + FP]
    x = xx[0:FP, :]
    for k in range(HALF):
        block = r[FP * k : FP * (k + 1)]
        total = total + block * xx[pl.ds(k, FP), :]
        acc[pl.ds(k, FP), :] += block * x
    total = total + acc[0:FP, :] + acc[F : F + FP, :]
    return jnp.where(field == F, 0.0, total)


def finish_first(g1, full, g1_ref):
    for k in range(HALF):
        pairs_to(g1, 0, k, F, full)
    row = lax.broadcasted_iota(jnp.int32, (8, 128), 0)
    lane = lax.broadcasted_iota(jnp.int32, (8, 128), 1)
    eye = jnp.where(row == lane, 1.0, 0.0).astype(BF)
    g1_ref[...] = dot(eye, full[pl.ds(0, F * F), :].astype(BF), 1, 1)


def finish_rest(t2, u_mine, w3_mine, w2_ref, full, tall, g2_ref, g3_ref):
    lane = lax.broadcasted_iota(jnp.int32, (H, 128), 1)
    for k in range(HALF):
        pairs_to(t2, 0, k, FP, full)
    full[pl.ds(F, F, stride=FP), :] = t2[pl.ds(FP * HALF, F), :]
    for i in range(F):
        block = jnp.concatenate([full[pl.ds(FP * i, FP), :], jnp.zeros((128 - FP, 128), F32)], axis=0)
        tall[pl.ds(i, H, stride=F), :] = jnp.transpose(block)
    flat = tall[...].astype(BF)
    g2_ref[...] = dot(u_mine, flat, 1, 1)
    v3 = dot(w2_ref[...], flat, 1, 0)
    for i in range(F):
        tall[pl.ds(i, H, stride=F), :] = jnp.where(lane == i, v3, 0.0)
    g3_ref[...] = dot(w3_mine, tall[...].astype(BF), 1, 1)


MESH = pl.DeviceIdType.MESH
T2ROWS = PL // 8


class Group:
    def __init__(self, n, me, device):
        self.n, self.me, self.device = n, me, device

    def others(self):
        return [lax.rem(self.me + r, self.n) for r in range(1, self.n)]

    def send(self, source, dst, sems):
        copies = []
        for r, p in enumerate(self.others()):
            copies.append(
                pltpu.make_async_remote_copy(
                    src_ref=source(p),
                    dst_ref=dst.at[self.me],
                    send_sem=sems.at[0, r],
                    recv_sem=sems.at[1, r],
                    device_id=self.device(p),
                    device_id_type=MESH,
                )
            )
            copies[-1].start()
        return copies


def arrived(copies):
    for c in copies:
        c.wait_recv()


def added(ref, n):
    total = ref[0].astype(F32)
    for p in range(1, n):
        total = total + ref[p].astype(F32)
    return total


def k_main(
    ids_ref, rows_ref, slots_ref, labels_ref, ow_ref, w1_ref, w2_ref, w3_ref,
    rg_ref, t2_ref, g1_ref, u_ref,
    w2, w3, tall, full, sym_q, sym_w, a_ref, at_ref, member, xx, z_ref, y_ref, acc,
    pooled, bags, sums, slots_out, slots_in, t2b, p1, px, py, p4, g1b, gx, gxs, gy, gz,
    load_sems, bag_sems, sum_sems, slot_sems, p1_sems, px_sems, py_sems, p4_sems, gx_sems, gy_sems, gz_sems,
):
    dp, samp, col = lax.axis_index("dp"), lax.axis_index("samp"), lax.axis_index("col")
    yy, xc = dp // 4, lax.rem(dp, 4)
    samps = Group(4, samp, lambda p: {"dp": dp, "samp": p, "col": col})
    cols = Group(2, col, lambda p: {"dp": dp, "samp": samp, "col": p})
    column = Group(8, samp * 2 + col, lambda p: {"dp": dp, "samp": p // 2, "col": lax.rem(p, 2)})
    alongx = Group(4, xc, lambda p: {"dp": yy * 4 + p, "samp": samp, "col": col})
    alongy = Group(4, yy, lambda p: {"dp": p * 4 + xc, "samp": samp, "col": col})

    loads = [
        pltpu.make_async_copy(w3_ref, w3, load_sems.at[0]),
        pltpu.make_async_copy(w2_ref, w2, load_sems.at[1]),
    ]
    for c in loads:
        c.start()
    barrier = pltpu.get_barrier_semaphore()
    for group in (column, alongx, alongy):
        for p in group.others():
            pl.semaphore_signal(barrier, inc=1, device_id=group.device(p), device_id_type=MESH)

    ids = ids_ref[...]
    member[...] = bag_member(ids)
    mine = pool(ids, rows_ref[0], member[...])
    pooled[...] = mine.reshape(4, 128, 128)
    bags[samp] = pooled[samp]
    pl.semaphore_wait(barrier, 13)
    started = samps.send(lambda p: pooled.at[p], bags, bag_sems)
    sent = started

    for c in loads:
        c.wait()
    prepare(w1_ref, w2, w3, ow_ref[...].astype(F32), tall, full, sym_q, sym_w, u_ref, a_ref, at_ref)

    arrived(started)
    x = gather_fields(slots_ref[...], bags[...].reshape(BAGS, 128))
    sums[col, :T2N] = forward(x, at_ref, xx, z_ref, y_ref)
    sums[col, T2N:] = jnp.zeros((16 - T2N, 128), F32)
    started = cols.send(lambda p: sums.at[col], sums, sum_sems)
    sent = sent + started
    grads = field_grads(a_ref, y_ref[...].astype(BF), xx, acc)
    arrived(started)
    slope = slope_row(sums[0, :T2N] + sums[1, :T2N], labels_ref)

    both = dot(z_ref[...], (y_ref[...] * slope).astype(BF), 1, 1)
    t2b[...] = both[:, :H].astype(BF).reshape(8, T2ROWS, 128)
    q = samp * 2 + col
    p1[q] = t2b[q]
    to_p1 = column.send(lambda p: t2b.at[p], p1, p1_sems)
    turned = jnp.concatenate([jnp.transpose(both[128 * b : 128 * (b + 1), H:]) for b in range(PL // 128)], axis=1)
    turned = jnp.concatenate([turned, jnp.zeros((H, 1024 - PL), F32)], axis=1)
    for d in range(16):
        block = turned[8 * d : 8 * d + 8]
        block = jnp.concatenate([block[:, :512], block[:, 512:]], axis=0).astype(BF)
        g1b[d % 4, d // 4] = block
    gx[xc] = g1b[xc]
    to_gx = alongx.send(lambda p: g1b.at[p], gx, gx_sems)
    slots_out[...] = scatter_fields(slots_ref[...], grads * slope).reshape(4, 128, 128)
    slots_in[samp] = slots_out[samp]
    to_slots = samps.send(lambda p: slots_out.at[p], slots_in, slot_sems)

    arrived(to_p1)
    px[xc] = added(p1, 8).astype(BF)
    to_px = alongx.send(lambda p: px.at[xc], px, px_sems)
    arrived(to_gx)
    gxs[...] = added(gx, 4).astype(BF)
    gy[yy] = gxs[yy]
    to_gy = alongy.send(lambda p: gxs.at[p], gy, gy_sems)
    arrived(to_px)
    py[yy] = added(px, 4).astype(BF)
    to_py = alongy.send(lambda p: py.at[yy], py, py_sems)
    arrived(to_slots)
    rg_ref[0] = spread_rows(ids, member[...], slots_in[...].reshape(BAGS, 128))
    arrived(to_gy)
    gz[q] = added(gy, 4).astype(BF)
    to_gz = column.send(lambda p: gz.at[q], gz, gz_sems)
    arrived(to_py)
    p4[q] = added(py, 4).astype(BF)
    to_p4 = column.send(lambda p: p4.at[q], p4, p4_sems)
    arrived(to_gz)
    block = added(gz, 8)
    g1_ref[...] = jnp.concatenate([block[:8], block[8:]], axis=1)
    arrived(to_p4)
    t2_ref[...] = p4[...].reshape(PL, 128).astype(F32)
    for c in sent + to_p1 + to_gx + to_slots + to_px + to_gy + to_py + to_gz + to_p4:
        c.wait_send()


def k_finish(t2_ref, g1_in, u_ref, ow_ref, w2_ref, g1_ref, g2_ref, g3_ref, full, tall, first):
    dp = lax.axis_index("dp")
    row = lax.broadcasted_iota(jnp.int32, (8, 128), 0)
    lane = lax.broadcasted_iota(jnp.int32, (8, 128), 1)
    mine = jnp.where(lane == row + 8 * dp, 1.0, 0.0).astype(BF)
    u_mine = dot(mine, u_ref[...], 1, 0).astype(BF)
    w3 = jnp.broadcast_to(ow_ref[2:3, :].astype(F32), (8, 128))
    w3 = jnp.sum(jnp.where(lane == row + 8 * dp, w3, 0.0), axis=1, keepdims=True)
    w3_mine = jnp.broadcast_to(w3, (8, 128)).astype(BF)
    tail = jnp.zeros((120, 128), F32)
    for b in range(PL // 128):
        block = jnp.concatenate([g1_in[:, 128 * b : 128 * (b + 1)], tail], axis=0)
        first[pl.ds(128 * b, 128), :] = jnp.transpose(block)
    finish_first(first, full, g1_ref)
    finish_rest(t2_ref, u_mine, w3_mine, w2_ref, full, tall, g2_ref, g3_ref)


def shape(dims, dtype):
    return jax.ShapeDtypeStruct(dims, dtype)


TALL = pltpu.VMEM((F * H, 128), F32)
FULL = pltpu.VMEM((F * FP, 128), F32)
ANY = pl.BlockSpec(memory_space=pl.ANY)


def pair_sems(n):
    return pltpu.SemaphoreType.DMA((2, n - 1))


def run_main(ids, rows, slots, labels, ow, w1, w2, w3):
    n = ids.shape[1]
    vm = pltpu.VMEM
    sym = vm((PL, 128), F32)
    scratch = [
        vm((H, F * H), BF), vm((H, F * H), BF), TALL, FULL, sym, sym,
        vm((PAIRS, 256), BF), vm((256, PL), BF), vm((BAGS, n), BF),
        vm((88, LANES), F32), vm((PL, LANES), BF), vm((256, LANES), F32), vm((88, LANES), F32),
        vm((4, 128, 128), BF), vm((4, 128, 128), BF), vm((2, 16, 128), F32),
        vm((4, 128, 128), BF), vm((4, 128, 128), BF),
        vm((8, T2ROWS, 128), BF), vm((8, T2ROWS, 128), BF), vm((4, T2ROWS, 128), BF), vm((4, T2ROWS, 128), BF), vm((8, T2ROWS, 128), BF),
        vm((4, 4, 16, 512), BF), vm((4, 4, 16, 512), BF), vm((4, 16, 512), BF), vm((4, 16, 512), BF), vm((8, 16, 512), BF),
        pltpu.SemaphoreType.DMA((2,)),
        pair_sems(4), pair_sems(2), pair_sems(4), pair_sems(8), pair_sems(4), pair_sems(4), pair_sems(8),
        pair_sems(4), pair_sems(4), pair_sems(8),
    ]
    return pl.pallas_call(
        k_main,
        out_shape=[shape((1, 64, n), BF), shape((PL, 128), F32), shape((8, 1024), F32), shape((H, 128), BF)],
        in_specs=[VMEM, VMEM, VMEM, SMEM, VMEM, VMEM, ANY, ANY],
        out_specs=[VMEM] * 4,
        scratch_shapes=scratch,
        compiler_params=pltpu.CompilerParams(collective_id=0, has_side_effects=True, vmem_limit_bytes=60 << 20),
    )(ids, rows, slots, labels, ow, w1, w2, w3)


def run_finish(t2, g1, u, ow, w2):
    return pl.pallas_call(
        k_finish,
        out_shape=[shape((8, F * F), F32), shape((8, F * H), F32), shape((8, F * H), F32)],
        in_specs=[VMEM] * 5,
        out_specs=[VMEM] * 3,
        scratch_shapes=[FULL, TALL, pltpu.VMEM((PL, 128), F32)],
        compiler_params=pltpu.CompilerParams(vmem_limit_bytes=60 << 20),
    )(t2, g1, u, ow, w2)


def local(looked_rows, bag_ids, slot_of, labels, out_weight, filter_first, filter_second, filter_third):
    rows, t2, g1, u = run_main(
        bag_ids, jnp.swapaxes(looked_rows, 1, 2), slot_of.reshape(1, FP), labels, out_weight,
        filter_first.T, filter_second, filter_third,
    )
    return (jnp.swapaxes(rows, 1, 2), *run_finish(t2, g1, u, out_weight, filter_second))


def solution(mesh):
    in_specs = (
        P(("dp", "samp"), None, "col"),
        P(("dp", "samp"), None),
        P(),
        P(("dp", "samp")),
        P(),
        P(),
        P(),
        P(),
    )
    out_specs = (P(("dp", "samp"), None, "col"), P("dp", None), P("dp", None), P("dp", None))
    return jax.shard_map(local, mesh=mesh, in_specs=in_specs, out_specs=out_specs, check_vma=False)
```

time: 201 us -> 43.2 us (0.21)
  waiting for transfers between devices: 137 us -> 0 us
  Pallas kernels: 25 us -> 41.7 us
  between operations: 14 us -> 0.65 us
  blocking collectives: 8.58 us -> 0 us
  starting transfers between devices: 8.41 us -> 0 us
  local copies, waits for them, and re-layouts: 5.53 us -> 0.7 us
    psum x1 -> x0, waiting for transfers between devices: 136 us -> none  [local(): weight = lax.psum(weight, ('dp', 'samp', 'col'))]
    pallas_call x6 -> x2, Pallas kernels: 25 us -> 41.7 us  [the longest x1 37.1 us: run_main(): pl.pallas_call(k_main, out_shape=[shape((1, 64, n), BF), shape((PL, 128),...]
    all_to_all x1 -> x0, blocking collectives: 8.58 us -> none  [local(): returned = lax.all_to_all(slot_grads, 'samp', 0, 0, tiled=True)]
    unnamed x7 -> x3, local copies, waits for them, and re-layouts: 5.53 us -> 0.7 us
    all_to_all x1 -> x0, starting transfers between devices: 4.72 us -> none  [local(): arrived = lax.all_to_all(pooled, 'samp', 0, 0, tiled=True)]
    ppermute x1 -> x0, starting transfers between devices: 3.7 us -> none  [local(): logits = sums + lax.ppermute(sums, 'col', [(0, 1), (1, 0)])]
  transfers between devices with their start and end apart: 3 -> 0, of which waited for: 2 -> 0; matrix products, arithmetic and copies ran while one was open for 1% -> 0% of each run, Pallas kernels for 4% -> 0%
where the time goes in v2:
time: 43.2 us; the launch traced here: 43 us
  Pallas kernels  41.7 us (97%)
  local copies, waits for them, and re-layouts  0.7 us (2%)
  between operations  0.65 us (2%)
    pallas_call x1, Pallas kernels, run_main(): pl.pallas_call(k_main, out_shape=[shape((1, 64, n), BF), shape((PL, 128),...  37.1 us
    pallas_call x1, Pallas kernels, run_finish(): pl.pallas_call(k_finish, out_shape=[shape((8, F * F), F32), shape((8, F *...  4.56 us

profile of v2, /device:TPU:1, one launch (start us, length us, event | category | flops | bytes accessed | tf_op | source)
XLA Modules:
  0.0 43.0 jit_solution(2740510602888403189)
XLA Ops:
  0.6 37.1 %shard_map.111 = (bf16[1,64,1920]{2,1,0:T(8,128)(2,1)}, f32[896,128]{1,0:T(8,128)}, f32[8,1024]{1,0:T(8,128)}, bf16[128,128]{1,0:T(8,128)(2,1)}) custom-call(s32[1,1920]{1,0:T(1,128)} %ids_ref.1, bf16[1,64,1920]{2,1,0:T(8,128)(2,1)} %bitcast.5, s32[1,40]{1,0:T(1,128)} %bitcast.7, s32[24]{0:T(128)} %labels_ref.1, bf16[3,128]{1,0:T(4,128)(2,1)} %ow_ref.3, ...), custom_call_target="tpu_custom_call" | custom-call | tf_op jit(solution)/shard_map/pallas_call | solution.py:401
  37.8 0.0 copy-start
  37.8 4.6 %shard_map.112 = (f32[8,1521]{1,0:T(8,128)}, f32[8,4992]{1,0:T(8,128)}, f32[8,4992]{1,0:T(8,128)}) custom-call(f32[896,128]{1,0:T(8,128)} %get-tuple-element.12.t2_ref, f32[8,1024]{1,0:T(8,128)} %get-tuple-element.13.g1_in, bf16[128,128]{1,0:T(8,128)(2,1)} %get-tuple-element.14.u_ref, bf16[3,128]{1,0:T(4,128)(2,1)} %ow_ref.3, bf16[128,4992]{1,0:T(8,128)(2,1)} %w2_ref.3), custom_call_target="tpu_custom_call" | custom-call | tf_op jit(solution)/shard_map/pallas_call | solution.py:412
  42.3 0.0 copy-done
  42.3 0.7 %copy.13 = bf16[1,1920,64]{1,2,0:T(8,128)(2,1)} copy(bf16[1,1920,64]{1,2,0:T(8,128)(2,1)S(1)} %bitcast.6) | data formatting | bytes 491520
Async XLA Ops:
  37.8 4.6 %copy-start = (bf16[1,64,1920]{2,1,0:T(8,128)(2,1)S(1)}, bf16[1,64,1920]{2,1,0:T(8,128)(2,1)}, u32[]{:S(2)}) copy-start(bf16[1,64,1920]{2,1,0:T(8,128)(2,1)} %get-tuple-element.11) | copy-start | bytes 737284

commit v3 on v2

v3 whole, which is shorter than its diff:
```python
import functools

import jax
import jax.numpy as jnp
from jax import lax
from jax.experimental import pallas as pl
from jax.experimental.pallas import tpu as pltpu
from jax.sharding import PartitionSpec as P

F = 39
FP = 40
H = 128
HALF = 20
PAIRS = 848
PL = 896
LANES = 1536
T2N = 12
BAGS = 512
CHUNK = 64
T2D = 6
SCALE = 16.0
BF = jnp.bfloat16
F32 = jnp.float32
VMEM = pl.BlockSpec(memory_space=pltpu.VMEM)
SMEM = pl.BlockSpec(memory_space=pltpu.SMEM)


def dot(a, b, ca, cb):
    return lax.dot_general(a, b, (((ca,), (cb,)), ((), ())), preferred_element_type=F32)


def lane_columns(row):
    n = row.shape[1] // 128
    blocks = [
        jnp.transpose(jnp.broadcast_to(row[:, b * 128 : (b + 1) * 128], (128, 128)))
        for b in range(n)
    ]
    return jnp.concatenate(blocks, axis=0)


def bag_places(ids):
    tens = (ids * 6554) >> 16
    twenties = (ids * 3277) >> 16
    row = twenties * 10 + (ids - tens * 10)
    row = row + 4 * ((row * 17477) >> 20)
    return row, tens - 2 * twenties


def bag_member(ids):
    place, _ = bag_places(ids)
    n = ids.shape[1]
    spot = lax.broadcasted_iota(jnp.int32, (BAGS, n), 0)
    return jnp.where(jnp.broadcast_to(place, (BAGS, n)) == spot, 1.0, 0.0).astype(BF)


def pool(ids, rows, member):
    half = bag_places(ids)[1].astype(F32)
    rows = rows.astype(F32)
    wide = jnp.concatenate([rows * (1.0 - half), rows * half], axis=0).astype(BF)
    return dot(member, wide, 1, 1).astype(BF)


def slot_row(slots):
    owner = (slots * 6554) >> 16
    base = owner * CHUNK + (slots - owner * 10)
    parts = [base + 10 * t for t in range(T2D)]
    parts.append(jnp.full((1, 256 - FP * T2D), -1, jnp.int32))
    return jnp.concatenate(parts, axis=1)


def gather_fields(slots, bags):
    col = lane_columns(slot_row(slots).astype(F32))[: FP * T2D]
    parts = []
    for b in range(2):
        lane = lax.broadcasted_iota(jnp.int32, col.shape, 1) + 128 * b
        parts.append(jnp.where(col == lane.astype(F32), 1.0, 0.0).astype(BF))
    chooser = jnp.concatenate(parts, axis=1)
    wide = jnp.concatenate([bags[:, h].reshape(4 * CHUNK, 128) for h in range(2)], axis=1)
    picked = dot(chooser, wide, 1, 0)
    x = jnp.concatenate([picked[FP * t : FP * (t + 1)] for t in range(T2D)], axis=1)
    field = lax.broadcasted_iota(jnp.int32, x.shape, 0)
    return jnp.where(field == F, 1.0, x)


def scatter_fields(slots, grads):
    row = slot_row(slots)
    spot = lax.broadcasted_iota(jnp.int32, (4 * CHUNK, 256), 0)
    member = jnp.where(jnp.broadcast_to(row, (4 * CHUNK, 256)) == spot, 1.0, 0.0).astype(BF)
    tall = [grads[:, 256 * t : 256 * (t + 1)] for t in range(T2D)]
    tall.append(jnp.zeros((256 - FP * T2D, 256), F32))
    both = dot(member, jnp.concatenate(tall, axis=0).astype(BF), 1, 0).astype(BF)
    return both[:, :128], both[:, 128:]


def spread_rows(ids, member, returned):
    half = bag_places(ids)[1]
    both = dot(returned, member, 0, 0)
    return jnp.where(half == 0, both[:64], both[64:]).astype(BF)


def pairs_from(full, k, stride, out, zero_tail=True):
    step = stride + 1
    low = full[pl.ds(k, F - k, stride=step), :]
    if k:
        low = low + full[pl.ds(k * stride, F - k, stride=step), :]
    out[pl.ds(FP * k, F - k), :] = low
    if k:
        high = full[pl.ds((F - k) * stride, k, stride=step), :]
        high = high + full[pl.ds(F - k, k, stride=step), :]
        out[pl.ds(FP * k + F - k, k), :] = high


def pairs_to(src, first, k, stride, full):
    step = stride + 1
    low = src[pl.ds(first + FP * k, F - k), :]
    full[pl.ds(k, F - k, stride=step), :] = low
    if k:
        full[pl.ds(k * stride, F - k, stride=step), :] = low
        high = src[pl.ds(first + FP * k + F - k, k), :]
        full[pl.ds((F - k) * stride, k, stride=step), :] = high
        full[pl.ds(F - k, k, stride=step), :] = high


def prepare_first(w1_ref, w3_ref, out_w, tall, full, sym_w, u_ref):
    lane = lax.broadcasted_iota(jnp.int32, (H, 128), 1)
    w3_col = lane_columns(out_w[2:3, :]).astype(BF)
    tall[...] = dot(w3_ref[...], w3_col, 0, 0)
    u = jnp.where(lane == F, lane_columns(out_w[1:2, :]), 0.0)
    for i in range(F):
        u = jnp.where(lane == i, tall[pl.ds(i, H, stride=F), :], u)
    u = u.astype(BF)
    u_ref[...] = u
    full[pl.ds(0, F * F), :] = w1_ref[...].astype(F32)
    sym_w[...] = jnp.zeros_like(sym_w)
    for k in range(HALF):
        pairs_from(full, k, F, sym_w)


def prepare_rest(w2_ref, out_w, tall, full, sym_q, sym_w, u_ref, w2p_ref, a_ref, at_ref):
    lane = lax.broadcasted_iota(jnp.int32, (H, 128), 1)
    sublane = lax.broadcasted_iota(jnp.int32, (H, 128), 0)
    tall[...] = dot(w2_ref[...], jnp.where(lane == sublane, 1.0, 0.0).astype(BF), 0, 0)
    for i in range(F):
        w2p_ref[pl.ds(H * i, H), :] = tall[pl.ds(i, H, stride=F), :].astype(BF)
    turned = jnp.transpose(u_ref[...].astype(F32))[:FP].astype(BF)
    blocks = dot(turned, w2p_ref[...], 1, 1)
    for i in range(F):
        full[pl.ds(FP * i, FP), :] = blocks[:, H * i : H * (i + 1)]
    sym_q[...] = jnp.zeros_like(sym_q)
    for k in range(HALF):
        pairs_from(full, k, FP, sym_q)
    sym_q[pl.ds(FP * HALF, F), :] = full[pl.ds(F, F, stride=FP), :]
    sym_q[pl.ds(FP * HALF + F, 1), :] = out_w[0:1, :]
    a_ref[:, :H] = sym_w[:PAIRS].astype(BF)
    a_ref[:, H:] = sym_q[:PAIRS].astype(BF)
    for b in range(PL // 128):
        at_ref[:H, 128 * b : 128 * (b + 1)] = jnp.transpose(sym_w[128 * b : 128 * (b + 1)]).astype(BF)
        at_ref[H:, 128 * b : 128 * (b + 1)] = jnp.transpose(sym_q[128 * b : 128 * (b + 1)]).astype(BF)


def forward(x, at_ref, xx, z_ref, y_ref):
    xx[0:FP, :] = x
    xx[F : F + FP, :] = x
    ones = xx[0:FP, :]
    field = lax.broadcasted_iota(jnp.int32, (FP, LANES), 0)
    x1 = jnp.where(field == F, 1.0, ones)
    for b in range(HALF // 2):
        two = [x1 * xx[pl.ds(k, FP), :] for k in (2 * b, 2 * b + 1)]
        z_ref[pl.ds(2 * FP * b, 2 * FP), :] = jnp.concatenate(two, axis=0).astype(BF)
    z_ref[pl.ds(FP * HALF, PL - FP * HALF), :] = jnp.concatenate(
        [x1, jnp.zeros((PL - FP * HALF - FP, LANES), F32)], axis=0
    ).astype(BF)
    y_ref[...] = dot(at_ref[...], z_ref[...], 1, 0)
    total = jnp.sum(y_ref[:H, :] * y_ref[H:, :], axis=0, keepdims=True)
    total = jnp.concatenate([total[:, 128 * t : 128 * (t + 1)] for t in range(T2N)], axis=0)
    total = jnp.concatenate(
        [total[2 * t : 2 * t + 1] + total[2 * t + 1 : 2 * t + 2] for t in range(T2D)], axis=0
    )
    first = lax.broadcasted_iota(jnp.int32, total.shape, 1) < 64
    low = jnp.sum(jnp.where(first, total, 0.0), axis=1, keepdims=True)
    high = jnp.sum(jnp.where(first, 0.0, total), axis=1, keepdims=True)
    return jnp.where(first, low, high)


def slope_row(logits, labels_ref, first):
    row = lax.broadcasted_iota(jnp.int32, logits.shape, 0)
    lane = lax.broadcasted_iota(jnp.int32, logits.shape, 1)
    sample = 2 * row + (lane >= 64).astype(jnp.int32)
    labels = jnp.zeros(logits.shape, F32)
    for n in range(2 * T2D):
        labels = jnp.where(sample == n, labels_ref[first + n].astype(F32), labels)
    slope = SCALE * (1.0 / (1.0 + jnp.exp(-logits)) - labels)
    return jnp.concatenate([slope[t // 2 : t // 2 + 1] for t in range(T2N)], axis=1)


def field_grads(a_ref, y16, xx, acc):
    swapped = jnp.concatenate([y16[H:], y16[:H]], axis=0)
    r = dot(a_ref[...], swapped, 1, 0)
    field = lax.broadcasted_iota(jnp.int32, (FP, LANES), 0)
    acc[...] = jnp.zeros_like(acc)
    total = r[FP * HALF : FP * HALF + FP]
    x = xx[0:FP, :]
    for k in range(HALF):
        block = r[FP * k : FP * (k + 1)]
        total = total + block * xx[pl.ds(k, FP), :]
        acc[pl.ds(k, FP), :] += block * x
    total = total + acc[0:FP, :] + acc[F : F + FP, :]
    return jnp.where(field == F, 0.0, total)


def finish_first(sums, mine, full, g1_ref):
    for k in range(HALF):
        pairs_to(sums, PAIRS, k, F, full)
    g1_ref[...] = dot(mine, full[pl.ds(0, F * F), :].astype(BF), 1, 1)


def finish_rest(t2, u_mine, w3_mine, w2p_ref, full, tall, g2_ref, g3_ref):
    for k in range(HALF):
        pairs_to(t2, 0, k, FP, full)
    full[pl.ds(F, F, stride=FP), :] = t2[pl.ds(FP * HALF, F), :]
    wide = jnp.concatenate([full[pl.ds(FP * i, FP), :] for i in range(F)], axis=1).astype(BF)
    two = dot(u_mine[:, :FP], wide, 1, 0)
    v3 = dot(wide, w2p_ref[...], 1, 0)
    rows = []
    for i in range(F):
        rows.append(two[:, H * i : H * (i + 1)])
        rows.append(w3_mine * v3[i : i + 1])
    rows.append(jnp.zeros((16, 128), F32))
    lane = lax.broadcasted_iota(jnp.int32, (H, 128), 1) // 16
    for b in range(5):
        block = jnp.transpose(jnp.concatenate(rows[16 * b : 16 * (b + 1)], axis=0))
        for i in range(8 * b, min(8 * b + 8, F)):
            tall[pl.ds(i, H, stride=F), :] = jnp.where(lane == i - 8 * b, block, 0.0)
    row = lax.broadcasted_iota(jnp.int32, (16, 128), 0)
    pick = jnp.where(lax.broadcasted_iota(jnp.int32, (16, 128), 1) % 16 == row, 1.0, 0.0).astype(BF)
    out = dot(pick, tall[...].astype(BF), 1, 1)
    g2_ref[...] = out[:8]
    g3_ref[...] = out[8:]


MESH = pl.DeviceIdType.MESH
SUMROWS = 1664
CUTS = (0, 512, 1024, SUMROWS)


class Group:
    def __init__(self, n, me, device):
        self.n, self.me, self.device = n, me, device

    def others(self):
        return [lax.rem(self.me + r, self.n) for r in range(1, self.n)]

    def send(self, source, dst, sems):
        copies = []
        for r, p in enumerate(self.others()):
            copies.append(
                pltpu.make_async_remote_copy(
                    src_ref=source(p),
                    dst_ref=dst.at[self.me],
                    send_sem=sems.at[0, r],
                    recv_sem=sems.at[1, r],
                    device_id=self.device(p),
                    device_id_type=MESH,
                )
            )
            copies[-1].start()
        return copies


def arrived(copies):
    for c in copies:
        c.wait_recv()


def added(ref, n):
    total = ref[0].astype(F32)
    for p in range(1, n):
        total = total + ref[p].astype(F32)
    return total


def k_main(
    ids_in, rows_in, slots_in_ref, labels_in, ow_in, w1_in, w2_in, w3_in,
    rg_out, w2p_out, sums_ref, um_ref, mine_ref, w3m_ref,
    ids_ref, rows_ref, slots_ref, labels_ref, ow_ref, w1_ref, w2, w3, tall, full, sym_q, sym_w, u_ref,
    w2p, rg, a_ref, at_ref, member, xx, z_ref, y_ref, acc,
    pooled, bags, slots_out, slots_in, *rest,
):
    parts = [rest[5 * i : 5 * i + 5] for i in range(3)]
    sems = [rest[15 + 4 * i : 19 + 4 * i] for i in range(3)]
    load_sems, store_sems, bag_sems, slot_sems = rest[27:]
    dp, samp, col = lax.axis_index("dp"), lax.axis_index("samp"), lax.axis_index("col")
    yy, xc = dp // 4, lax.rem(dp, 4)
    zz, core = col * 2 + samp // 2, lax.rem(samp, 2)
    q = samp * 2 + col

    def device(x=xc, y=yy, z=zz, c=core):
        return {"dp": y * 4 + x, "samp": lax.rem(z, 2) * 2 + c, "col": z // 2}

    column = Group(8, q, lambda p: {"dp": dp, "samp": p // 2, "col": lax.rem(p, 2)})
    x4 = Group(4, xc, lambda p: device(x=p))
    y4 = Group(4, yy, lambda p: device(y=p))
    z4 = Group(4, zz, lambda p: device(z=p))
    x8 = Group(8, xc * 2 + core, lambda p: device(x=p // 2, c=lax.rem(p, 2)))
    y8 = Group(8, yy * 2 + core, lambda p: device(y=p // 2, c=lax.rem(p, 2)))
    z8 = Group(8, zz * 2 + core, lambda p: device(z=p // 2, c=lax.rem(p, 2)))
    orders = ((z8, x4, y4), (x8, y4, z4), (y8, z4, x4))

    barrier = pltpu.get_barrier_semaphore()
    for p in column.others():
        pl.semaphore_signal(barrier, inc=1, device_id=column.device(p), device_id_type=MESH)
    for r in range(1, 4):
        for c in range(2):
            for peer in (device(x=lax.rem(xc + r, 4), c=c), device(y=lax.rem(yy + r, 4), c=c)):
                pl.semaphore_signal(barrier, inc=1, device_id=peer, device_id_type=MESH)
    loads = []
    for n, (source, target) in enumerate((
        (ids_in, ids_ref), (rows_in, rows_ref), (ow_in, ow_ref), (w3_in, w3), (w1_in, w1_ref), (w2_in, w2),
        (slots_in_ref, slots_ref), (labels_in, labels_ref),
    )):
        loads.append(pltpu.make_async_copy(source, target, load_sems.at[n]))
        loads[-1].start()
    loads[0].wait()
    loads[1].wait()

    ids = ids_ref[...]
    member[...] = bag_member(ids)
    pooled[...] = pool(ids, rows_ref[0], member[...]).reshape(8, CHUNK, 128)
    bags[q] = pooled[q]
    for c in loads[2:]:
        c.wait()
    out_w = ow_ref[...].astype(F32)
    prepare_first(w1_ref, w3, out_w, tall, full, sym_w, u_ref)
    pl.semaphore_wait(barrier, 19)
    to_bags = column.send(lambda p: pooled.at[p], bags, bag_sems)
    prepare_rest(w2, out_w, tall, full, sym_q, sym_w, u_ref, w2p, a_ref, at_ref)
    stores = [pltpu.make_async_copy(w2p, w2p_out, store_sems.at[0])]
    stores[0].start()
    row = lax.broadcasted_iota(jnp.int32, (8, 128), 0)
    lane = lax.broadcasted_iota(jnp.int32, (8, 128), 1)
    mine = jnp.where(lane == row + 8 * dp, 1.0, 0.0)
    mine_ref[...] = mine
    um_ref[...] = dot(mine.astype(BF), u_ref[...], 1, 0)
    w3_mine = jnp.sum(mine * out_w[2:3, :], axis=1, keepdims=True)
    w3m_ref[...] = jnp.broadcast_to(w3_mine, (8, 128))

    arrived(to_bags)
    x = gather_fields(slots_ref[...], bags[...].reshape(4, 2, CHUNK, 128))
    slope = slope_row(forward(x, at_ref, xx, z_ref, y_ref), labels_ref, 12 * col)
    both = dot(z_ref[...], (y_ref[...] * slope).astype(BF), 1, 1)
    flat = jnp.concatenate(
        [both[:PAIRS, :H], both[: FP * HALF, H:], jnp.zeros((SUMROWS - PAIRS - FP * HALF, 128), F32)], axis=0
    ).astype(BF)
    sent = list(to_bags)
    flying = []
    for i, (part, order) in enumerate(zip(parts, orders)):
        whole, landed = part[0], part[1]
        whole[...] = flat[CUTS[i] : CUTS[i + 1]].reshape(whole.shape)
        landed[order[0].me] = whole[order[0].me]
        flying.append(order[0].send(lambda p, whole=whole: whole.at[p], landed, sems[i][0]))
    grads = field_grads(a_ref, y_ref[...].astype(BF), xx, acc) * slope
    halves = scatter_fields(slots_ref[...], grads)
    for owner in range(4):
        for h in range(2):
            slots_out[2 * owner + h] = halves[h][CHUNK * owner : CHUNK * (owner + 1)]
    slots_in[q] = slots_out[q]
    to_slots = column.send(lambda p: slots_out.at[p], slots_in, slot_sems)
    sent = sent + to_slots

    for stage in range(1, 4):
        if stage == 3:
            arrived(to_slots)
        for i, (part, order) in enumerate(zip(parts, orders)):
            arrived(flying[i])
            sent = sent + flying[i]
            group = order[stage] if stage < 3 else order[0]
            source, landed = part[stage], part[stage + 1]
            landed[group.me] = added(source, 8 if stage == 1 else 4).astype(BF)
            flying[i] = group.send(lambda p, landed=landed, me=group.me: landed.at[me], landed, sems[i][stage])
    rg[0] = spread_rows(ids, member[...], slots_in[...].reshape(BAGS, 128))
    stores.append(pltpu.make_async_copy(rg, rg_out, store_sems.at[1]))
    stores[1].start()
    for i, part in enumerate(parts):
        arrived(flying[i])
        sent = sent + flying[i]
        sums_ref[pl.ds(CUTS[i], CUTS[i + 1] - CUTS[i]), :] = part[4][...].reshape(CUTS[i + 1] - CUTS[i], 128)
    for c in stores:
        c.wait()
    for c in sent:
        c.wait_send()


def shape(dims, dtype):
    return jax.ShapeDtypeStruct(dims, dtype)


TALL = pltpu.VMEM((F * H, 128), F32)
FULL = pltpu.VMEM((F * FP, 128), F32)
ANY = pl.BlockSpec(memory_space=pl.ANY)


def pair_sems(n):
    return pltpu.SemaphoreType.DMA((2, n - 1))


def run_main(ids, rows, slots, labels, ow, w1, w2, w3):
    n = ids.shape[1]
    vm = pltpu.VMEM
    sym = vm((PL, 128), F32)
    scratch = [
        vm(ids.shape, jnp.int32), vm(rows.shape, BF), vm(slots.shape, jnp.int32), pltpu.SMEM(labels.shape, jnp.int32),
        vm(ow.shape, BF), vm(w1.shape, BF), vm((H, F * H), BF), vm((H, F * H), BF), TALL, FULL, sym, sym, vm((H, 128), BF),
        vm((F * H, 128), BF), vm((1, 64, n), BF), vm((PAIRS, 256), BF), vm((256, PL), BF), vm((BAGS, n), BF),
        vm((88, LANES), F32), vm((PL, LANES), BF), vm((256, LANES), F32), vm((88, LANES), F32),
        vm((8, CHUNK, 128), BF), vm((8, CHUNK, 128), BF), vm((8, CHUNK, 128), BF), vm((8, CHUNK, 128), BF),
    ]
    for low, high in zip(CUTS, CUTS[1:]):
        scratch += [vm((k, (high - low) // 8, 128), BF) for k in (8, 8, 4, 4, 8)]
    scratch += [pair_sems(k) for _ in range(3) for k in (8, 4, 4, 8)]
    scratch += [pltpu.SemaphoreType.DMA((8,)), pltpu.SemaphoreType.DMA((2,)), pair_sems(8), pair_sems(8)]
    return pl.pallas_call(
        k_main,
        out_shape=[
            shape((1, 64, n), BF), shape((F * H, 128), BF), shape((SUMROWS, 128), BF),
            shape((8, 128), F32), shape((8, 128), F32), shape((8, 128), F32),
        ],
        in_specs=[ANY] * 8,
        out_specs=[ANY, ANY] + [VMEM] * 4,
        scratch_shapes=scratch,
        compiler_params=pltpu.CompilerParams(collective_id=0, has_side_effects=True, vmem_limit_bytes=58 << 20),
    )(ids, rows, slots, labels, ow, w1, w2, w3)


def k_finish(
    rows_in, w2p_in, sums_in, um_ref, mine_ref, w3m_ref,
    rg_out, g1_ref, g2_ref, g3_ref,
    full, tall, sums, w2p, rows, sems,
):
    copies = [
        pltpu.make_async_copy(w2p_in, w2p, sems.at[0]),
        pltpu.make_async_copy(rows_in, rows, sems.at[1]),
        pltpu.make_async_copy(rows, rg_out, sems.at[2]),
    ]
    for c in copies[:2]:
        c.start()
    sums[...] = sums_in[...].astype(F32)
    finish_first(sums, mine_ref[...].astype(BF), full, g1_ref)
    copies[1].wait()
    copies[2].start()
    copies[0].wait()
    finish_rest(sums, um_ref[...].astype(BF), w3m_ref[...], w2p, full, tall, g2_ref, g3_ref)
    copies[2].wait()


def run_finish(rows, w2p, sums, um, mine, w3m):
    return pl.pallas_call(
        k_finish,
        out_shape=[
            shape(rows.shape, BF), shape((8, F * F), F32), shape((8, F * H), F32), shape((8, F * H), F32)
        ],
        in_specs=[ANY, ANY] + [VMEM] * 4,
        out_specs=[ANY] + [VMEM] * 3,
        scratch_shapes=[
            FULL, TALL, pltpu.VMEM(sums.shape, F32), pltpu.VMEM(w2p.shape, BF),
            pltpu.VMEM(rows.shape, BF), pltpu.SemaphoreType.DMA((3,)),
        ],
        compiler_params=pltpu.CompilerParams(vmem_limit_bytes=60 << 20),
    )(rows, w2p, sums, um, mine, w3m)


def local(looked_rows, bag_ids, slot_of, labels, out_weight, filter_first, filter_second, filter_third):
    parts = run_main(
        bag_ids, jnp.swapaxes(looked_rows, 1, 2), slot_of.reshape(1, FP), labels, out_weight,
        filter_first.T, filter_second, filter_third,
    )
    rows, first, second, third = run_finish(*parts)
    return jnp.swapaxes(rows, 1, 2), first, second, third


def solution(mesh):
    in_specs = (
        P(("dp", "samp"), None, "col"),
        P(("dp", "samp"), None),
        P(),
        P(("dp", "samp")),
        P(),
        P(),
        P(),
        P(),
    )
    out_specs = (P(("dp", "samp"), None, "col"), P("dp", None), P("dp", None), P("dp", None))
    return jax.shard_map(local, mesh=mesh, in_specs=in_specs, out_specs=out_specs, check_vma=False)
```

time: 43.2 us -> 39.2 us (0.907)
  Pallas kernels: 41.7 us -> 38.4 us
  local copies, waits for them, and re-layouts: 0.7 us -> 0 us
    pallas_call x2, Pallas kernels: 41.7 us -> 38.4 us  [the longest x1 34.2 us: run_main(): pl.pallas_call(k_main, out_shape=[shape((1, 64, n), BF), shape((F * H, 12...]
    unnamed x3 -> x0, local copies, waits for them, and re-layouts: 0.7 us -> none
where the time goes in v3:
time: 39.2 us; the launch traced here: 39.1 us
  Pallas kernels  38.4 us (98%)
  between operations  0.64 us (2%)
    pallas_call x1, Pallas kernels, run_main(): pl.pallas_call(k_main, out_shape=[shape((1, 64, n), BF), shape((F * H, 12...  34.2 us
    pallas_call x1, Pallas kernels, run_finish(): pl.pallas_call(k_finish, out_shape=[shape(rows.shape, BF), shape((8, F *...  4.21 us

profile of v3, /device:TPU:1, one launch (start us, length us, event | category | flops | bytes accessed | tf_op | source)
XLA Modules:
  0.0 39.1 jit_solution(13304129779928987448)
XLA Ops:
  0.6 34.2 %shard_map.111 = (bf16[1,64,1920]{2,1,0:T(8,128)(2,1)}, bf16[4992,128]{1,0:T(8,128)(2,1)}, bf16[1664,128]{1,0:T(8,128)(2,1)}, f32[8,128]{1,0:T(8,128)}, f32[8,128]{1,0:T(8,128)}, /*index=5*/f32[8,128]{1,0:T(8,128)}) custom-call(s32[1,1920]{1,0:T(1,128)} %ids_in.1, bf16[1,64,1920]{2,1,0:T(8,128)(2,1)} %bitcast.5, s32[1,40]{1,0:T(1,128)} %bitcast.6, ...), custom_call_target="tpu_custom_call" | custom-call | tf_op jit(solution)/shard_map/pallas_call | solution.py:421
  34.9 4.2 %shard_map.112 = (bf16[1,64,1920]{2,1,0:T(8,128)(2,1)}, f32[8,1521]{1,0:T(8,128)}, f32[8,4992]{1,0:T(8,128)}, f32[8,4992]{1,0:T(8,128)}) custom-call(bf16[1,64,1920]{2,1,0:T(8,128)(2,1)} %get-tuple-element.14.rows_in, bf16[4992,128]{1,0:T(8,128)(2,1)} %get-tuple-element.15.w2p_in, bf16[1664,128]{1,0:T(8,128)(2,1)} %get-tuple-element.16.sums_in, ...), custom_call_target="tpu_custom_call" | custom-call | tf_op jit(solution)/shard_map/pallas_call | solution.py:456

commit v4 on v3

--- a/solution.py
+++ b/solution.py
@@ -68,13 +68,16 @@
     return jnp.concatenate(parts, axis=1)
 
 
-def gather_fields(slots, bags):
+def field_chooser(slots):
     col = lane_columns(slot_row(slots).astype(F32))[: FP * T2D]
     parts = []
     for b in range(2):
         lane = lax.broadcasted_iota(jnp.int32, col.shape, 1) + 128 * b
         parts.append(jnp.where(col == lane.astype(F32), 1.0, 0.0).astype(BF))
-    chooser = jnp.concatenate(parts, axis=1)
+    return jnp.concatenate(parts, axis=1)
+
+
+def gather_fields(chooser, bags):
     wide = jnp.concatenate([bags[:, h].reshape(4 * CHUNK, 128) for h in range(2)], axis=1)
     picked = dot(chooser, wide, 1, 0)
     x = jnp.concatenate([picked[FP * t : FP * (t + 1)] for t in range(T2D)], axis=1)
@@ -281,14 +284,14 @@
 
 def k_main(
     ids_in, rows_in, slots_in_ref, labels_in, ow_in, w1_in, w2_in, w3_in,
-    rg_out, w2p_out, sums_ref, um_ref, mine_ref, w3m_ref,
+    rg, w2p, sums_ref, um_ref, mine_ref, w3m_ref,
     ids_ref, rows_ref, slots_ref, labels_ref, ow_ref, w1_ref, w2, w3, tall, full, sym_q, sym_w, u_ref,
-    w2p, rg, a_ref, at_ref, member, xx, z_ref, y_ref, acc,
-    pooled, bags, slots_out, slots_in, *rest,
+    a_ref, at_ref, member, xx, z_ref, y_ref, acc,
+    pooled, bags, slots_out, slots_in, chooser_ref, *rest,
 ):
     parts = [rest[5 * i : 5 * i + 5] for i in range(3)]
     sems = [rest[15 + 4 * i : 19 + 4 * i] for i in range(3)]
-    load_sems, store_sems, bag_sems, slot_sems = rest[27:]
+    load_sems, bag_sems, slot_sems = rest[27:]
     dp, samp, col = lax.axis_index("dp"), lax.axis_index("samp"), lax.axis_index("col")
     yy, xc = dp // 4, lax.rem(dp, 4)
     zz, core = col * 2 + samp // 2, lax.rem(samp, 2)
@@ -327,15 +330,13 @@
     member[...] = bag_member(ids)
     pooled[...] = pool(ids, rows_ref[0], member[...]).reshape(8, CHUNK, 128)
     bags[q] = pooled[q]
+    pl.semaphore_wait(barrier, 19)
+    to_bags = column.send(lambda p: pooled.at[p], bags, bag_sems)
     for c in loads[2:]:
         c.wait()
     out_w = ow_ref[...].astype(F32)
     prepare_first(w1_ref, w3, out_w, tall, full, sym_w, u_ref)
-    pl.semaphore_wait(barrier, 19)
-    to_bags = column.send(lambda p: pooled.at[p], bags, bag_sems)
     prepare_rest(w2, out_w, tall, full, sym_q, sym_w, u_ref, w2p, a_ref, at_ref)
-    stores = [pltpu.make_async_copy(w2p, w2p_out, store_sems.at[0])]
-    stores[0].start()
     row = lax.broadcasted_iota(jnp.int32, (8, 128), 0)
     lane = lax.broadcasted_iota(jnp.int32, (8, 128), 1)
     mine = jnp.where(lane == row + 8 * dp, 1.0, 0.0)
@@ -344,8 +345,9 @@
     w3_mine = jnp.sum(mine * out_w[2:3, :], axis=1, keepdims=True)
     w3m_ref[...] = jnp.broadcast_to(w3_mine, (8, 128))
 
+    chooser_ref[...] = field_chooser(slots_ref[...])
     arrived(to_bags)
-    x = gather_fields(slots_ref[...], bags[...].reshape(4, 2, CHUNK, 128))
+    x = gather_fields(chooser_ref[...], bags[...].reshape(4, 2, CHUNK, 128))
     slope = slope_row(forward(x, at_ref, xx, z_ref, y_ref), labels_ref, 12 * col)
     both = dot(z_ref[...], (y_ref[...] * slope).astype(BF), 1, 1)
     flat = jnp.concatenate(
@@ -378,14 +380,10 @@
             landed[group.me] = added(source, 8 if stage == 1 else 4).astype(BF)
             flying[i] = group.send(lambda p, landed=landed, me=group.me: landed.at[me], landed, sems[i][stage])
     rg[0] = spread_rows(ids, member[...], slots_in[...].reshape(BAGS, 128))
-    stores.append(pltpu.make_async_copy(rg, rg_out, store_sems.at[1]))
-    stores[1].start()
     for i, part in enumerate(parts):
         arrived(flying[i])
         sent = sent + flying[i]
         sums_ref[pl.ds(CUTS[i], CUTS[i + 1] - CUTS[i]), :] = part[4][...].reshape(CUTS[i + 1] - CUTS[i], 128)
-    for c in stores:
-        c.wait()
     for c in sent:
         c.wait_send()
 
@@ -410,46 +408,33 @@
     scratch = [
         vm(ids.shape, jnp.int32), vm(rows.shape, BF), vm(slots.shape, jnp.int32), pltpu.SMEM(labels.shape, jnp.int32),
         vm(ow.shape, BF), vm(w1.shape, BF), vm((H, F * H), BF), vm((H, F * H), BF), TALL, FULL, sym, sym, vm((H, 128), BF),
-        vm((F * H, 128), BF), vm((1, 64, n), BF), vm((PAIRS, 256), BF), vm((256, PL), BF), vm((BAGS, n), BF),
+        vm((PAIRS, 256), BF), vm((256, PL), BF), vm((BAGS, n), BF),
         vm((88, LANES), F32), vm((PL, LANES), BF), vm((256, LANES), F32), vm((88, LANES), F32),
         vm((8, CHUNK, 128), BF), vm((8, CHUNK, 128), BF), vm((8, CHUNK, 128), BF), vm((8, CHUNK, 128), BF),
+        vm((FP * T2D, 256), BF),
     ]
     for low, high in zip(CUTS, CUTS[1:]):
         scratch += [vm((k, (high - low) // 8, 128), BF) for k in (8, 8, 4, 4, 8)]
     scratch += [pair_sems(k) for _ in range(3) for k in (8, 4, 4, 8)]
-    scratch += [pltpu.SemaphoreType.DMA((8,)), pltpu.SemaphoreType.DMA((2,)), pair_sems(8), pair_sems(8)]
+    scratch += [pltpu.SemaphoreType.DMA((8,)), pair_sems(8), pair_sems(8)]
     return pl.pallas_call(
         k_main,
         out_shape=[
-            shape((1, 64, n), BF), shape((F * H, 128), BF), shape((SUMROWS, 128), BF),
-            shape((8, 128), F32), shape((8, 128), F32), shape((8, 128), F32),
+            vm((1, 64, n), BF), vm((F * H, 128), BF), vm((SUMROWS, 128), BF),
+            vm((8, 128), F32), vm((8, 128), F32), vm((8, 128), F32),
         ],
         in_specs=[ANY] * 8,
-        out_specs=[ANY, ANY] + [VMEM] * 4,
+        out_specs=[VMEM] * 6,
         scratch_shapes=scratch,
-        compiler_params=pltpu.CompilerParams(collective_id=0, has_side_effects=True, vmem_limit_bytes=58 << 20),
+        compiler_params=pltpu.CompilerParams(collective_id=0, has_side_effects=True, vmem_limit_bytes=53 << 20),
     )(ids, rows, slots, labels, ow, w1, w2, w3)
 
 
-def k_finish(
-    rows_in, w2p_in, sums_in, um_ref, mine_ref, w3m_ref,
-    rg_out, g1_ref, g2_ref, g3_ref,
-    full, tall, sums, w2p, rows, sems,
-):
-    copies = [
-        pltpu.make_async_copy(w2p_in, w2p, sems.at[0]),
-        pltpu.make_async_copy(rows_in, rows, sems.at[1]),
-        pltpu.make_async_copy(rows, rg_out, sems.at[2]),
-    ]
-    for c in copies[:2]:
-        c.start()
+def k_finish(rows_in, w2p, sums_in, um_ref, mine_ref, w3m_ref, rg_ref, g1_ref, g2_ref, g3_ref, full, tall, sums):
+    rg_ref[...] = rows_in[...]
     sums[...] = sums_in[...].astype(F32)
     finish_first(sums, mine_ref[...].astype(BF), full, g1_ref)
-    copies[1].wait()
-    copies[2].start()
-    copies[0].wait()
     finish_rest(sums, um_ref[...].astype(BF), w3m_ref[...], w2p, full, tall, g2_ref, g3_ref)
-    copies[2].wait()
 
 
 def run_finish(rows, w2p, sums, um, mine, w3m):
@@ -458,13 +443,10 @@
         out_shape=[
             shape(rows.shape, BF), shape((8, F * F), F32), shape((8, F * H), F32), shape((8, F * H), F32)
         ],
-        in_specs=[ANY, ANY] + [VMEM] * 4,
-        out_specs=[ANY] + [VMEM] * 3,
-        scratch_shapes=[
-            FULL, TALL, pltpu.VMEM(sums.shape, F32), pltpu.VMEM(w2p.shape, BF),
-            pltpu.VMEM(rows.shape, BF), pltpu.SemaphoreType.DMA((3,)),
-        ],
-        compiler_params=pltpu.CompilerParams(vmem_limit_bytes=60 << 20),
+        in_specs=[VMEM] * 6,
+        out_specs=[VMEM] * 4,
+        scratch_shapes=[FULL, TALL, pltpu.VMEM(sums.shape, F32)],
+        compiler_params=pltpu.CompilerParams(vmem_limit_bytes=30 << 20),
     )(rows, w2p, sums, um, mine, w3m)
 
 

time: 39.2 us -> 35 us (0.89)
  Pallas kernels: 38.4 us -> 34.2 us
    pallas_call x1, Pallas kernels: 4.21 us -> 2.02 us  [run_finish(): pl.pallas_call(k_finish, out_shape=[shape(rows.shape, BF), shape((8, F *...]
    pallas_call x1, Pallas kernels: 34.2 us -> 32.2 us  [run_main(): pl.pallas_call(k_main, out_shape=[vm((1, 64, n), BF), vm((F * H, 128), BF...]
where the time goes in v4:
time: 35 us; the launch traced here: 34.9 us
  Pallas kernels  34.2 us (98%)
  between operations  0.64 us (2%)
    pallas_call x1, Pallas kernels, run_main(): pl.pallas_call(k_main, out_shape=[vm((1, 64, n), BF), vm((F * H, 128), BF...  32.2 us
    pallas_call x1, Pallas kernels, run_finish(): pl.pallas_call(k_finish, out_shape=[shape(rows.shape, BF), shape((8, F *...  2.02 us

profile of v4, /device:TPU:1, one launch (start us, length us, event | category | flops | bytes accessed | tf_op | source)
XLA Modules:
  0.0 34.9 jit_solution(14843804669384060397)
XLA Ops:
  0.6 32.2 %shard_map.111 = (bf16[1,64,1920]{2,1,0:T(8,128)(2,1)S(1)}, bf16[4992,128]{1,0:T(8,128)(2,1)S(1)}, bf16[1664,128]{1,0:T(8,128)(2,1)S(1)}, f32[8,128]{1,0:T(8,128...) custom-call(s32[1,1920]{1,0:T(1,128)} %ids_in.1, bf16[1,64,1920]{2,1,0:T(8,128)(2,1)} %bitcast.5, s32[1,40]{1,0:T(1,128)} %bitcast.6, ...), custom_call_target="tpu_custom_call" | custom-call | tf_op jit(solution)/shard_map/pallas_call | solution.py:420
  32.8 2.0 %shard_map.112 = (bf16[1,64,1920]{2,1,0:T(8,128)(2,1)}, f32[8,1521]{1,0:T(8,128)}, f32[8,4992]{1,0:T(8,128)}, f32[8,4992]{1,0:T(8,128)}) custom-call(bf16[1,64,1920]{2,1,0:T(8,128)(2,1)S(1)} %get-tuple-element.14.rows_in, bf16[4992,128]{1,0:T(8,128)(2,1)S(1)} %get-tuple-element.15.w2p, bf16[1664,128]{1,0:T(8,128)(2,1)S(1)} %get-tuple-element.16.sums_in, ...), custom_call_target="tpu_custom_call" | custom-call | tf_op jit(solution)/shard_map/pallas_call | solution.py:441

commit v5 on v4

--- a/solution.py
+++ b/solution.py
@@ -243,6 +243,7 @@
 
 MESH = pl.DeviceIdType.MESH
 SUMROWS = 1664
+ZCUTS = (0, 256, 512, PAIRS)
 CUTS = (0, 512, 1024, SUMROWS)
 
 
@@ -309,6 +310,14 @@
     z8 = Group(8, zz * 2 + core, lambda p: device(z=p // 2, c=lax.rem(p, 2)))
     orders = ((z8, x4, y4), (x8, y4, z4), (y8, z4, x4))
 
+    loads = []
+    for n, (source, target) in enumerate((
+        (ids_in, ids_ref), (rows_in, rows_ref), (ow_in, ow_ref), (w3_in, w3), (w1_in, w1_ref), (w2_in, w2),
+        (slots_in_ref, slots_ref), (labels_in, labels_ref),
+    )):
+        loads.append(pltpu.make_async_copy(source, target, load_sems.at[n]))
+    for c in loads[:2]:
+        c.start()
     barrier = pltpu.get_barrier_semaphore()
     for p in column.others():
         pl.semaphore_signal(barrier, inc=1, device_id=column.device(p), device_id_type=MESH)
@@ -316,13 +325,8 @@
         for c in range(2):
             for peer in (device(x=lax.rem(xc + r, 4), c=c), device(y=lax.rem(yy + r, 4), c=c)):
                 pl.semaphore_signal(barrier, inc=1, device_id=peer, device_id_type=MESH)
-    loads = []
-    for n, (source, target) in enumerate((
-        (ids_in, ids_ref), (rows_in, rows_ref), (ow_in, ow_ref), (w3_in, w3), (w1_in, w1_ref), (w2_in, w2),
-        (slots_in_ref, slots_ref), (labels_in, labels_ref),
-    )):
-        loads.append(pltpu.make_async_copy(source, target, load_sems.at[n]))
-        loads[-1].start()
+    for c in loads[2:]:
+        c.start()
     loads[0].wait()
     loads[1].wait()
 
@@ -349,15 +353,18 @@
     arrived(to_bags)
     x = gather_fields(chooser_ref[...], bags[...].reshape(4, 2, CHUNK, 128))
     slope = slope_row(forward(x, at_ref, xx, z_ref, y_ref), labels_ref, 12 * col)
-    both = dot(z_ref[...], (y_ref[...] * slope).astype(BF), 1, 1)
-    flat = jnp.concatenate(
-        [both[:PAIRS, :H], both[: FP * HALF, H:], jnp.zeros((SUMROWS - PAIRS - FP * HALF, 128), F32)], axis=0
-    ).astype(BF)
+    scaled = (y_ref[...] * slope).astype(BF)
     sent = list(to_bags)
     flying = []
     for i, (part, order) in enumerate(zip(parts, orders)):
         whole, landed = part[0], part[1]
-        whole[...] = flat[CUTS[i] : CUTS[i + 1]].reshape(whole.shape)
+        low, high = ZCUTS[i], ZCUTS[i + 1]
+        both = dot(z_ref[low:high], scaled, 1, 1)
+        rows = [both[:, :H], both[: min(high, FP * HALF) - low, H:]]
+        left = CUTS[i + 1] - CUTS[i] - sum(r.shape[0] for r in rows)
+        if left:
+            rows.append(jnp.zeros((left, 128), F32))
+        whole[...] = jnp.concatenate(rows, axis=0).astype(BF).reshape(whole.shape)
         landed[order[0].me] = whole[order[0].me]
         flying.append(order[0].send(lambda p, whole=whole: whole.at[p], landed, sems[i][0]))
     grads = field_grads(a_ref, y_ref[...].astype(BF), xx, acc) * slope
@@ -430,11 +437,18 @@
     )(ids, rows, slots, labels, ow, w1, w2, w3)
 
 
-def k_finish(rows_in, w2p, sums_in, um_ref, mine_ref, w3m_ref, rg_ref, g1_ref, g2_ref, g3_ref, full, tall, sums):
-    rg_ref[...] = rows_in[...]
-    sums[...] = sums_in[...].astype(F32)
+def k_finish(rows_in, w2p, sums_in, um_ref, mine_ref, w3m_ref, rg_out, g1_ref, g2_ref, g3_ref, full, tall, sums, sem):
+    rows = pltpu.make_async_copy(rows_in, rg_out, sem)
+    rows.start()
+    for i in range(3):
+        low, high = ZCUTS[i], ZCUTS[i + 1]
+        top = min(high, FP * HALF)
+        sums[low:high, :] = sums_in[CUTS[i] : CUTS[i] + high - low, :].astype(F32)
+        first = CUTS[i] + high - low
+        sums[PAIRS + low : PAIRS + top, :] = sums_in[first : first + top - low, :].astype(F32)
     finish_first(sums, mine_ref[...].astype(BF), full, g1_ref)
     finish_rest(sums, um_ref[...].astype(BF), w3m_ref[...], w2p, full, tall, g2_ref, g3_ref)
+    rows.wait()
 
 
 def run_finish(rows, w2p, sums, um, mine, w3m):
@@ -444,8 +458,8 @@
             shape(rows.shape, BF), shape((8, F * F), F32), shape((8, F * H), F32), shape((8, F * H), F32)
         ],
         in_specs=[VMEM] * 6,
-        out_specs=[VMEM] * 4,
-        scratch_shapes=[FULL, TALL, pltpu.VMEM(sums.shape, F32)],
+        out_specs=[ANY] + [VMEM] * 3,
+        scratch_shapes=[FULL, TALL, pltpu.VMEM(sums.shape, F32), pltpu.SemaphoreType.DMA(())],
         compiler_params=pltpu.CompilerParams(vmem_limit_bytes=30 << 20),
     )(rows, w2p, sums, um, mine, w3m)
 

time: 35 us -> 34.2 us (0.977)
  Pallas kernels: 34.2 us -> 33.4 us
    pallas_call x1, Pallas kernels: 32.2 us -> 31.4 us  [run_main(): pl.pallas_call(k_main, out_shape=[vm((1, 64, n), BF), vm((F * H, 128), BF...]
where the time goes in v5:
time: 34.2 us; the launch traced here: 34.1 us
  Pallas kernels  33.4 us (98%)
  between operations  0.64 us (2%)
    pallas_call x1, Pallas kernels, run_main(): pl.pallas_call(k_main, out_shape=[vm((1, 64, n), BF), vm((F * H, 128), BF...  31.4 us
    pallas_call x1, Pallas kernels, run_finish(): pl.pallas_call(k_finish, out_shape=[shape(rows.shape, BF), shape((8, F *...  2.03 us

profile of v5, /device:TPU:1, one launch (start us, length us, event | category | flops | bytes accessed | tf_op | source)
XLA Modules:
  0.0 34.1 jit_solution(18202185767135606169)
XLA Ops:
  0.6 31.4 %shard_map.111 = (bf16[1,64,1920]{2,1,0:T(8,128)(2,1)S(1)}, bf16[4992,128]{1,0:T(8,128)(2,1)S(1)}, bf16[1664,128]{1,0:T(8,128)(2,1)S(1)}, f32[8,128]{1,0:T(8,128...) custom-call(s32[1,1920]{1,0:T(1,128)} %ids_in.1, bf16[1,64,1920]{2,1,0:T(8,128)(2,1)} %bitcast.5, s32[1,40]{1,0:T(1,128)} %bitcast.6, ...), custom_call_target="tpu_custom_call" | custom-call | tf_op jit(solution)/shard_map/pallas_call | solution.py:427
  32.0 2.0 %shard_map.112 = (bf16[1,64,1920]{2,1,0:T(8,128)(2,1)}, f32[8,1521]{1,0:T(8,128)}, f32[8,4992]{1,0:T(8,128)}, f32[8,4992]{1,0:T(8,128)}) custom-call(bf16[1,64,1920]{2,1,0:T(8,128)(2,1)S(1)} %get-tuple-element.14.rows_in, bf16[4992,128]{1,0:T(8,128)(2,1)S(1)} %get-tuple-element.15.w2p, bf16[1664,128]{1,0:T(8,128)(2,1)S(1)} %get-tuple-element.16.sums_in, ...), custom_call_target="tpu_custom_call" | custom-call | tf_op jit(solution)/shard_map/pallas_call | solution.py:455
